TPU v7x, 128 devices: a whole 4x4x4 slice. The times are simulated.
128 devices in a mesh: dp: 16 (over x, y), ep: 8 (over z, core).
Axes of the slice: x: 4, y: 4, z: 4, core: 2. Of those that a mesh axis runs over, the one named last changes fastest.
Arguments:
- queries_c: bfloat16 [2048, 32768], P('dp', 'ep'), may hold values from -17 to 17
- queries_r: bfloat16 [2048, 4096], P('dp', 'ep'), may hold values from -17 to 17
- latents: bfloat16 [2048, 512], P('dp'), may hold values from -4 to 4
- key_rope: bfloat16 [64, 2048], P(None, 'dp'), may hold values from -4 to 4
- value_up: bfloat16 [64, 512, 128], P('ep'), may hold values from -0.25 to 0.25
- out_proj: bfloat16 [8192, 3584], P('ep'), may hold values from -0.0625 to 0.0625
- norm_gain: float32 [3584], replicated, may hold values from 0.1 to 1.9
- router: bfloat16 [3584, 16], replicated, may hold values from -0.09375 to 0.09375
- gate_up: bfloat16 [16, 2, 3584, 2048], P('dp', None, None, 'ep'), may hold values from -0.09375 to 0.09375
- down: bfloat16 [16, 2048, 3584], P('dp', 'ep'), may hold values from -0.125 to 0.125
- routes: int32 [2048, 2], P(('dp', 'ep')), may hold values from 0 to 15, all different within a row; in each aligned block of 16 rows (0 to 15, 16 to 31, ...) at most 2 rows name the same one
- lengths: int32 [16], replicated, may hold values from 32 to 128, as said below
- plan: int32 [16], replicated, may hold values from 0 to 15, as said below
Outputs:
- layer_out: bfloat16 [2048, 3584], P(('dp', 'ep'))
Inputs may be any that keep to these rules, and one draw needn't show every extreme that they name: Prompt r fills positions 0 to lengths[r] - 1 of its buffer; some prompt fills all 128; half of the prompts reach into their last block and the other half are at most 64 long. A permutation of the ranks that pairs them: the last 16 positions of prompt r are processed on rank plan[r], plan[plan[r]] = r and plan[r] != r; the k-th shortest prompt is paired with the k-th longest (ties broken by rank). `routes`: each row names 2 different experts; within the rows of one device (16 aligned rows) no expert is named more than 2 times.
All inputs are finite; a program needn't handle non-finite values.
Results may differ from a plain program's by a relative error of at most 0.033.
Values may be sent and summed in bfloat16 or wider, within the bound.
A program may use at most 64 MiB of HBM per device.

v0:
```python
import jax
import jax.numpy as jnp
from jax import lax
from jax.sharding import PartitionSpec as P

LAT = 512
ROPE = 64
VDIM = 128
S = 128
SPAN = 16


softmax_scale = 192.0 ** (-0.5)
route_scale = 2.5
norm_eps = 1e-06


def attend(queries, rotary, latent_rows, key_rotary, positions, length):
    scores = jnp.einsum("ihc,jc->hij", queries, latent_rows, preferred_element_type=jnp.float32)
    scores = (
        scores + jnp.einsum("ihd,dj->hij", rotary, key_rotary, preferred_element_type=jnp.float32)
    ) * softmax_scale
    places = jnp.arange(latent_rows.shape[0], dtype=jnp.int32)
    visible = (places[None, :] <= positions[:, None]) & (places[None, :] < length)
    highest = jnp.max(jnp.where(visible[None], scores, -jnp.inf), axis=2, keepdims=True)
    weights = jnp.where(visible[None], jnp.exp(scores - highest), 0.0)
    totals = jnp.sum(weights, axis=2)
    mixed = jnp.einsum(
        "hij,jc->ihc", weights.astype(jnp.bfloat16), latent_rows, preferred_element_type=jnp.float32
    )
    mixed = mixed / jnp.transpose(totals)[:, :, None]
    return jnp.where((positions < length)[:, None, None], mixed, 0.0).astype(jnp.bfloat16)


def pair_slots(route_rows, experts, capacity):
    flat = route_rows.reshape(-1)
    onehot = (flat[:, None] == jnp.arange(experts, dtype=jnp.int32)[None, :]).astype(jnp.int32)
    before = jnp.cumsum(onehot, axis=0) - onehot
    position = jnp.sum(before * onehot, axis=1)
    return flat * capacity + position


def place_matrix(slots, experts, capacity, rows, fanout):
    target = jnp.arange(experts * capacity, dtype=jnp.int32)
    return jnp.any(slots.reshape(rows, fanout)[None, :, :] == target[:, None, None], axis=2)


def slot_out(array, picked):
    shaped = picked.reshape((picked.shape[0],) + (1,) * array.ndim)
    return jnp.where(shaped, array[None], jnp.zeros((), array.dtype))


def expert_apply(rows_in, gate_up, down):
    gate = jnp.dot(rows_in, gate_up[0, 0], preferred_element_type=jnp.float32)
    upper = jnp.dot(rows_in, gate_up[0, 1], preferred_element_type=jnp.float32)
    hidden = (jax.nn.silu(gate) * upper).astype(jnp.bfloat16)
    return jnp.dot(hidden, down[0], preferred_element_type=jnp.float32)


def per_device(
    queries_c,
    queries_r,
    latents,
    key_rope,
    value_up,
    out_proj,
    norm_gain,
    router,
    gate_up,
    down,
    routes,
    lengths,
    plan,
):
    rank_count = lax.axis_size("dp")
    shard_count = lax.axis_size("ep")
    own_rank = lax.axis_index("dp")
    heads_here = queries_r.shape[1] // ROPE
    keep_rows = S - SPAN
    rank_ids = jnp.arange(rank_count, dtype=jnp.int32)
    source = jnp.sum(jnp.where(plan == own_rank, rank_ids, 0))
    own_length = lengths[own_rank]
    source_length = lengths[source]
    picked = rank_ids == plan[own_rank]
    arrived = (
        lax.all_to_all(
            slot_out(queries_c[keep_rows:], picked), "dp", split_axis=0, concat_axis=0, tiled=True
        ),
        lax.all_to_all(
            slot_out(queries_r[keep_rows:], picked), "dp", split_axis=0, concat_axis=0, tiled=True
        ),
        lax.all_to_all(slot_out(latents, picked), "dp", split_axis=0, concat_axis=0, tiled=True),
        lax.all_to_all(slot_out(key_rope, picked), "dp", split_axis=0, concat_axis=0, tiled=True),
    )
    moved_c = lax.dynamic_index_in_dim(arrived[0], source, 0, keepdims=False)
    moved_r = lax.dynamic_index_in_dim(arrived[1], source, 0, keepdims=False)
    moved_lat = lax.dynamic_index_in_dim(arrived[2], source, 0, keepdims=False)
    moved_key = lax.dynamic_index_in_dim(arrived[3], source, 0, keepdims=False)
    own_part = attend(
        queries_c[:keep_rows].reshape(keep_rows, heads_here, LAT),
        queries_r[:keep_rows].reshape(keep_rows, heads_here, ROPE),
        latents,
        key_rope,
        jnp.arange(keep_rows, dtype=jnp.int32),
        own_length,
    )
    moved_part = attend(
        moved_c.reshape(SPAN, heads_here, LAT),
        moved_r.reshape(SPAN, heads_here, ROPE),
        moved_lat,
        moved_key,
        jnp.arange(keep_rows, S, dtype=jnp.int32),
        source_length,
    )
    placed = jnp.concatenate([own_part, moved_part], axis=0)
    values = jnp.einsum(
        "ihc,hcv->ihv", placed, value_up, preferred_element_type=jnp.float32
    ).astype(jnp.bfloat16)
    values = values.reshape(S, heads_here * VDIM)
    row_count = routes.shape[0]
    fanout = routes.shape[1]
    mixed = lax.psum_scatter(
        jnp.dot(values, out_proj, preferred_element_type=jnp.float32).astype(jnp.bfloat16),
        "ep",
        scatter_dimension=0,
        tiled=True,
    ).astype(jnp.float32)
    normed = (
        mixed * lax.rsqrt(jnp.mean(mixed * mixed, axis=1, keepdims=True) + norm_eps) * norm_gain
    ).astype(jnp.bfloat16)
    logits = jnp.dot(normed, router, preferred_element_type=jnp.float32)
    chosen = jax.nn.sigmoid(jnp.take_along_axis(logits, routes, axis=1))
    route_weights = route_scale * chosen / jnp.sum(chosen, axis=1, keepdims=True)
    capacity = 5 * row_count * fanout // (4 * rank_count)
    slots = pair_slots(routes, rank_count, capacity)
    places = place_matrix(slots, rank_count, capacity, row_count, fanout).astype(jnp.bfloat16)
    outgoing = jnp.dot(places, normed, preferred_element_type=jnp.float32).astype(jnp.bfloat16)
    outgoing = outgoing.reshape(rank_count, capacity, -1)
    width = outgoing.shape[2]
    copies = jnp.broadcast_to(outgoing[:, None], (rank_count, shard_count, capacity, width))
    copies = copies.reshape(rank_count * shard_count, capacity, width)
    received = lax.all_to_all(copies, ("dp", "ep"), split_axis=0, concat_axis=0, tiled=True)
    partial_value = expert_apply(received.reshape(-1, width), gate_up, down).astype(jnp.bfloat16)
    partial_value = partial_value.reshape(rank_count * shard_count, capacity, width)
    returned = lax.all_to_all(partial_value, ("dp", "ep"), split_axis=0, concat_axis=0, tiled=True)
    expert_out = jnp.sum(
        returned.reshape(rank_count, shard_count, capacity, width).astype(jnp.float32), axis=1
    )
    pair_out = jnp.take(expert_out.reshape(rank_count * capacity, width), slots, axis=0)
    pair_out = pair_out.reshape(row_count, fanout, width)
    combined = mixed + jnp.sum(route_weights[:, :, None] * pair_out, axis=1)
    return combined.astype(jnp.bfloat16)


def solution(mesh):
    placed = (
        P("dp", "ep"),
        P("dp", "ep"),
        P("dp", None),
        P(None, "dp"),
        P("ep", None, None),
        P("ep", None),
        P(),
        P(),
        P("dp", None, None, "ep"),
        P("dp", "ep", None),
        P(("dp", "ep"), None),
        P(),
        P(),
    )
    return jax.shard_map(
        per_device, mesh=mesh, in_specs=placed, out_specs=P(("dp", "ep"), None), check_vma=False
    )
```

profile of v0, /device:TPU:1, one launch (start us, length us, event | category | flops | bytes accessed | tf_op | source)
XLA Modules:
  0.0 245.0 jit_solution(12170326311727258792)
XLA Ops:
  6.5 1.4 dynamic_slice.27
  7.9 0.6 iota_compare_fusion.5
  8.6 0.7 slice.21
  9.3 0.8 broadcast_select_fusion.2
  10.1 7.6 %all-to-all-start.3 = ((bf16[16,16,512]{2,1,0:T(8,128)(2,1)}), bf16[16,16,512]{2,1,0:T(8,128)(2,1)S(1)}, u32[]{:S(2)}, u32[]{:S(2)}) async-start(bf16[16,16,512]{2,1,0:T(8,128)(2,1)} %broadcast_select_fusion.2), calls=%async_computation.3 | async-start | bytes 524288 | tf_op jit(solution)/shard_map/all_to_all | solution.py:89
  17.7 0.9 slice.20
  18.6 1.5 broadcast_select_fusion
  20.1 5.0 %all-to-all-done.3 = bf16[16,16,512]{2,1,0:T(8,128)(2,1)S(1)} async-done(((bf16[16,16,512]{2,1,0:T(8,128)(2,1)}), bf16[16,16,512]{2,1,0:T(8,128)(2,1)S(1)}, u32[]{:S(2)}, u32[]{:S(2)}) %all-to-all-start.3) | async-done | bytes 262176 | tf_op jit(solution)/shard_map/all_to_all | solution.py:89
  25.1 4.4 %all-to-all-start.1 = ((bf16[16,16,4096]{2,1,0:T(8,128)(2,1)}), bf16[16,16,4096]{2,1,0:T(8,128)(2,1)}, u32[]{:S(2)}, u32[]{:S(2)}) async-start(bf16[16,16,4096]{2,1,0:T(8,128)(2,1)} %broadcast_select_fusion), calls=%async_computation.1 | async-start | bytes 4194304 | tf_op jit(solution)/shard_map/all_to_all | solution.py:86
  29.6 0.6 fusion.83
  32.3 0.6 fusion.95
  32.9 0.6 iota_compare_fusion.4
  33.5 0.6 broadcast_compare_fusion
  34.2 0.7 iota_compare_fusion.6
  34.8 1.5 broadcast_select_fusion.1
  36.4 18.9 %all-to-all-done.1 = bf16[16,16,4096]{2,1,0:T(8,128)(2,1)} async-done(((bf16[16,16,4096]{2,1,0:T(8,128)(2,1)}), bf16[16,16,4096]{2,1,0:T(8,128)(2,1)}, u32[]{:S(2)}, u32[]{:S(2)}) %all-to-all-start.1) | async-done | bytes 2097184 | tf_op jit(solution)/shard_map/all_to_all | solution.py:86
  55.3 5.2 %all-to-all-start = ((bf16[16,128,512]{2,1,0:T(8,128)(2,1)}), bf16[16,128,512]{2,1,0:T(8,128)(2,1)}, u32[]{:S(2)}, u32[]{:S(2)}) async-start(bf16[16,128,512]{2,1,0:T(8,128)(2,1)} %broadcast_select_fusion.1), calls=%async_computation | async-start | bytes 4194304 | tf_op jit(solution)/shard_map/all_to_all | solution.py:92
  60.6 0.7 iota_compare_fusion.7
  61.3 0.8 broadcast_select_fusion.3
  62.1 0.4 fusion.35
  62.5 0.3 fusion.12
  62.8 0.4 fusion.97
  63.2 1.3 fusion.8
  64.6 20.9 %all-to-all-done = bf16[16,128,512]{2,1,0:T(8,128)(2,1)} async-done(((bf16[16,128,512]{2,1,0:T(8,128)(2,1)}), bf16[16,128,512]{2,1,0:T(8,128)(2,1)}, u32[]{:S(2)}, u32[]{:S(2)}) %all-to-all-start) | async-done | bytes 2097184 | tf_op jit(solution)/shard_map/all_to_all | solution.py:92
  85.5 5.3 %all-to-all-start.2 = ((bf16[16,64,128]{2,1,0:T(8,128)(2,1)}), bf16[16,64,128]{2,1,0:T(8,128)(2,1)S(1)}, u32[]{:S(2)}, u32[]{:S(2)}) async-start(bf16[16,64,128]{2,1,0:T(8,128)(2,1)} %broadcast_select_fusion.3), calls=%async_computation.2 | async-start | bytes 524288 | tf_op jit(solution)/shard_map/all_to_all | solution.py:93
  90.9 0.9 constant_dynamic-slice_fusion.1
  91.9 1.1 fusion.52
  93.0 5.2 %all-to-all-done.2 = bf16[16,64,128]{2,1,0:T(8,128)(2,1)S(1)} async-done(((bf16[16,64,128]{2,1,0:T(8,128)(2,1)}), bf16[16,64,128]{2,1,0:T(8,128)(2,1)S(1)}, u32[]{:S(2)}, u32[]{:S(2)}) %all-to-all-start.2) | async-done | bytes 262176 | tf_op jit(solution)/shard_map/all_to_all | solution.py:93
  98.5 1.2 fusion.21
  99.7 1.7 convolution_convert_fusion.3
  101.5 5.2 %convolution_convert_fusion.1 = bf16[128,3584]{1,0:T(8,128)(2,1)} fusion(bf16[128,1024]{0,1:T(8,128)(2,1)S(1)} %bitcast.92, bf16[1024,3584]{1,0:T(8,128)(2,1)} %param.18), kind=kOutput, calls=%fused_computation.5 | convolution fusion | flops 939982848 | bytes 8519680 | tf_op jit(solution)/shard_map/dot_general | solution.py:123
  107.4 32.8 %reduce-scatter.2.cloned.1.call-done = bf16[16,3584]{1,0:T(8,128)(2,1)} async-done(((bf16[128,3584]{1,0:T(8,128)(2,1)}), bf16[16,3584]{1,0:T(8,128)(2,1)}) %reduce-scatter.2.cloned.1.call-update) | async-done | bytes 114704 | tf_op jit(solution)/shard_map/reduce_scatter | solution.py:122
  140.2 1.0 fusion.44
  141.3 1.2 convolution_convert_fusion.2
  142.6 0.9 broadcast_in_dim.217
  143.5 37.5 %all_to_all.30 = bf16[128,2,3584]{2,1,0:T(2,128)(2,1)} all-to-all(bf16[128,2,3584]{2,1,0:T(2,128)(2,1)S(1)} %bitcast.90), channel_id=1, replica_groups=mesh['dp'=16,'ep'=8] {'dp','ep'}, dimensions={0} | all-to-all | bytes 3670016 | tf_op jit(solution)/shard_map/all_to_all | solution.py:142
  181.0 5.0 %reshape.227 = bf16[256,3584]{1,0:T(8,128)(2,1)} reshape(bf16[128,2,3584]{2,1,0:T(2,128)(2,1)} %all_to_all.30) | data formatting | bytes 3670016 | tf_op jit(solution)/shard_map/reshape | solution.py:143
  185.9 2.7 %fusion.5 = f32[256,256]{1,0:T(8,128)S(1)} fusion(bf16[256,3584]{1,0:T(8,128)(2,1)} %reshape.227, bf16[1,2,3584,256]{3,2,1,0:T(8,128)(2,1)} %param.21), kind=kOutput, calls=%fused_computation.13 | convolution fusion | flops 469762048 | bytes 3932160 | tf_op jit(solution)/shard_map/dot_general | solution.py:54
  188.6 5.4 %convolution_convert_fusion = bf16[256,3584]{1,0:T(8,128)(2,1)} fusion(bf16[1,256,3584]{2,1,0:T(8,128)(2,1)S(1)} %copy-done, bf16[256,3584]{1,0:T(8,128)(2,1)} %reshape.227, bf16[1,2,3584,256]{3,2,1,0:T(8,128)(2,1)} %param.21, f32[256,256]{1,0:T(8,128)S(1)} %fusion.5), kind=kOutput, calls=%fused_computation.4 | convolution fusion | flops 940834816 | bytes 7602176 | tf_op jit(solution)/shard_map/dot_general | solution.py:57
  194.0 4.8 %reshape.228 = bf16[128,2,3584]{2,1,0:T(2,128)(2,1)} reshape(bf16[256,3584]{1,0:T(8,128)(2,1)} %convolution_convert_fusion) | data formatting | bytes 3670016 | tf_op jit(solution)/shard_map/reshape | solution.py:144
  198.8 5.7 %all-to-all-start.5 = ((bf16[128,2,3584]{2,1,0:T(2,128)(2,1)}), bf16[128,2,3584]{2,1,0:T(2,128)(2,1)}, u32[]{:S(2)}, u32[]{:S(2)}) async-start(bf16[128,2,3584]{2,1,0:T(2,128)(2,1)} %reshape.228), calls=%async_computation.6 | async-start | bytes 3670016 | tf_op jit(solution)/shard_map/all_to_all | solution.py:145
  205.3 0.7 gather_fusion.1
  206.3 25.8 %all-to-all-done.5 = bf16[128,2,3584]{2,1,0:T(2,128)(2,1)} async-done(((bf16[128,2,3584]{2,1,0:T(2,128)(2,1)}), bf16[128,2,3584]{2,1,0:T(2,128)(2,1)}, u32[]{:S(2)}, u32[]{:S(2)}) %all-to-all-start.5) | async-done | bytes 1835040 | tf_op jit(solution)/shard_map/all_to_all | solution.py:145
  232.1 3.3 %convert_reduce_fusion = f32[16,2,3584]{2,1,0:T(2,128)S(1)} fusion(bf16[128,2,3584]{2,1,0:T(2,128)(2,1)} %all-to-all-done.5), kind=kLoop, calls=%fused_computation.7 | loop fusion | flops 1720320 | bytes 2293760 | tf_op jit(solution)/shard_map/reduce_sum | solution.py:146
  235.4 0.3 reshape.229
  235.8 0.7 gather_fusion
  236.8 0.7 multiply_reduce_fusion
  237.5 0.7 fusion.47
  (62 shorter events, 2.8 us)
Async XLA Ops:
  6.5 182.1 %copy-start = (bf16[1,256,3584]{2,1,0:T(8,128)(2,1)S(1)}, bf16[1,256,3584]{2,1,0:T(8,128)(2,1)}, u32[]{:S(2)}) copy-start(bf16[1,256,3584]{2,1,0:T(8,128)(2,1)} %param.22) | copy-start | bytes 5505028
  10.1 15.0 %all-to-all-start.3 = ((bf16[16,16,512]{2,1,0:T(8,128)(2,1)}), bf16[16,16,512]{2,1,0:T(8,128)(2,1)S(1)}, u32[]{:S(2)}, u32[]{:S(2)}) async-start(bf16[16,16,512]{2,1,0:T(8,128)(2,1)} %broadcast_select_fusion.2), calls=%async_computation.3 | async-start | bytes 524288 | tf_op jit(solution)/shard_map/all_to_all | solution.py:89
  20.1 9.5 %copy-start.8 = (s32[16]{0:T(128)S(1)}, s32[16]{0:T(128)}, u32[]{:S(2)}) copy-start(s32[16]{0:T(128)} %param.25) | copy-start | bytes 196
  20.1 11.4 %slice-start.1 = ((bf16[128,512]{1,0:T(8,128)(2,1)}), bf16[112,512]{1,0:T(8,128)(2,1)S(1)}, s32[]{:S(2)}) async-start(bf16[128,512]{1,0:T(8,128)(2,1)} %param.14), calls=%async_computation.9 | async-start | bytes 229376 | tf_op jit(solution)/shard_map/slice | solution.py:101
  25.1 30.2 %all-to-all-start.1 = ((bf16[16,16,4096]{2,1,0:T(8,128)(2,1)}), bf16[16,16,4096]{2,1,0:T(8,128)(2,1)}, u32[]{:S(2)}, u32[]{:S(2)}) async-start(bf16[16,16,4096]{2,1,0:T(8,128)(2,1)} %broadcast_select_fusion), calls=%async_computation.1 | async-start | bytes 4194304 | tf_op jit(solution)/shard_map/all_to_all | solution.py:86
  29.6 2.7 %copy-start.6 = (s32[16]{0:T(128)S(1)}, s32[16]{0:T(128)}, u32[]{:S(2)}) copy-start(s32[16]{0:T(128)} %param.24) | copy-start | bytes 196
  29.6 5.3 %copy-start.2 = (bf16[128,512]{1,0:T(8,128)(2,1)S(1)}, bf16[128,512]{1,0:T(8,128)(2,1)}, u32[]{:S(2)}) copy-start(bf16[128,512]{1,0:T(8,128)(2,1)} %param.15) | copy-start | bytes 393220
  36.4 24.9 %copy-start.3 = (bf16[64,128]{1,0:T(8,128)(2,1)S(1)}, bf16[64,128]{1,0:T(8,128)(2,1)}, u32[]{:S(2)}) copy-start(bf16[64,128]{1,0:T(8,128)(2,1)} %param.16) | copy-start | bytes 49156
  36.4 25.7 %slice-start = ((bf16[128,4096]{1,0:T(8,128)(2,1)}), bf16[112,4096]{1,0:T(8,128)(2,1)S(1)}, s32[]{:S(2)}) async-start(bf16[128,4096]{1,0:T(8,128)(2,1)} %param.13), calls=%async_computation.8 | async-start | bytes 1835008 | tf_op jit(solution)/shard_map/slice | solution.py:100
  55.3 30.2 %all-to-all-start = ((bf16[16,128,512]{2,1,0:T(8,128)(2,1)}), bf16[16,128,512]{2,1,0:T(8,128)(2,1)}, u32[]{:S(2)}, u32[]{:S(2)}) async-start(bf16[16,128,512]{2,1,0:T(8,128)(2,1)} %broadcast_select_fusion.1), calls=%async_computation | async-start | bytes 4194304 | tf_op jit(solution)/shard_map/all_to_all | solution.py:92
  64.5 35.2 %copy-start.9 = (bf16[112,8,512]{2,0,1:T(8,128)(2,1)S(1)}, bf16[112,8,512]{2,0,1:T(8,128)(2,1)}, u32[]{:S(2)}) copy-start(bf16[112,8,512]{2,0,1:T(8,128)(2,1)} %fusion.8) | copy-start | bytes 2752516
  85.5 12.7 %all-to-all-start.2 = ((bf16[16,64,128]{2,1,0:T(8,128)(2,1)}), bf16[16,64,128]{2,1,0:T(8,128)(2,1)S(1)}, u32[]{:S(2)}, u32[]{:S(2)}) async-start(bf16[16,64,128]{2,1,0:T(8,128)(2,1)} %broadcast_select_fusion.3), calls=%async_computation.2 | async-start | bytes 524288 | tf_op jit(solution)/shard_map/all_to_all | solution.py:93
  90.9 49.3 %reduce-scatter.2.cloned.1.call-start = ((), (), s32[]{:S(2)}) async-start(), calls=%async_computation.7 | async-start | bytes 1032192 | tf_op jit(solution)/shard_map/reduce_scatter | solution.py:122
  101.4 5.2 %copy-start.4 = (s32[16,2]{0,1:T(2,128)S(1)}, s32[16,2]{0,1:T(2,128)}, u32[]{:S(2)}) copy-start(s32[16,2]{0,1:T(2,128)} %param.23) | copy-start | bytes 388
  101.4 39.8 %copy-start.5 = (f32[3584]{0:T(1024)S(1)}, f32[3584]{0:T(1024)}, u32[]{:S(2)}) copy-start(f32[3584]{0:T(1024)} %param.19) | copy-start | bytes 43012
  198.8 6.3 %copy-start.1 = (bf16[16,3584]{1,0:T(8,128)(2,1)S(1)}, bf16[16,3584]{1,0:T(8,128)(2,1)}, u32[]{:S(2)}) copy-start(bf16[16,3584]{1,0:T(8,128)(2,1)} %reduce-scatter.2.cloned.1.call-done) | copy-start | bytes 344068
  198.8 6.3 %copy-start.7 = (bf16[3584,16]{0,1:T(8,128)(2,1)S(1)}, bf16[3584,16]{0,1:T(8,128)(2,1)}, u32[]{:S(2)}) copy-start(bf16[3584,16]{0,1:T(8,128)(2,1)} %param.20) | copy-start | bytes 344068
  198.8 33.3 %all-to-all-start.5 = ((bf16[128,2,3584]{2,1,0:T(2,128)(2,1)}), bf16[128,2,3584]{2,1,0:T(2,128)(2,1)}, u32[]{:S(2)}, u32[]{:S(2)}) async-start(bf16[128,2,3584]{2,1,0:T(2,128)(2,1)} %reshape.228), calls=%async_computation.6 | async-start | bytes 3670016 | tf_op jit(solution)/shard_map/all_to_all | solution.py:145
Sparse Core Ops, SparseCore 0:
  106.8 33.4 reduce-scatter.1
where the time goes:
time: 246 us; the launch traced here: 245 us
  waiting for transfers between devices  109 us (44%)
  blocking collectives  37.5 us (15%)
  starting transfers between devices  28.4 us (12%)
  matrix products  20.7 us (8%)
  local copies, waits for them, and re-layouts  18.7 us (8%)
  between operations  15.8 us (6%)
  other arithmetic  15.3 us (6%)
    all_to_all x1, blocking collectives, per_device(): lax.all_to_all(copies, ('dp', 'ep'), split_axis=0, concat_axis=0, tiled=T...  37.5 us
    reduce_scatter x1, waiting for transfers between devices, per_device(): lax.psum_scatter(jnp.dot(values, out_proj, preferred_element_type=jnp.flo...  32.8 us
    all_to_all x1, waiting for transfers between devices, per_device(): lax.all_to_all(partial_value, ('dp', 'ep'), split_axis=0, concat_axis=0,...  25.8 us
    all_to_all x1, waiting for transfers between devices, per_device(): lax.all_to_all(slot_out(latents, picked), 'dp', split_axis=0, concat_axis...  20.9 us
    all_to_all x1, waiting for transfers between devices, per_device(): lax.all_to_all(slot_out(queries_c[keep_rows:], picked), 'dp', split_axis=...  18.9 us
    all_to_all x1, starting transfers between devices, per_device(): lax.all_to_all(slot_out(queries_r[keep_rows:], picked), 'dp', split_axis=...  7.58 us
    all_to_all x1, starting transfers between devices, per_device(): lax.all_to_all(partial_value, ('dp', 'ep'), split_axis=0, concat_axis=0,...  5.75 us
    dot_general x1, matrix products, expert_apply(): return jnp.dot(hidden, down[0], preferred_element_type=jnp.float32)  5.39 us
  transfers between devices with their start and end apart: 6, of which 6 were waited for; matrix products, arithmetic and copies ran while one was open for 6% of the time, Pallas kernels for 0%

commit v1 on v0

v1 whole, which is shorter than its diff:
```python
import jax
import jax.numpy as jnp
from jax import lax
from jax.experimental import pallas as pl
from jax.experimental.pallas import tpu as pltpu
from jax.sharding import PartitionSpec as P

MESH = pl.DeviceIdType.MESH
BF = jnp.bfloat16
F32 = jnp.float32

D = 3584
LAT = 512
ROPE = 64
VDIM = 128
S = 128
SPAN = 16
HEADS_HERE = 8
N_DP = 16
N_Z = 4
HALF = 64
COLS = D // N_Z
SLOTS = 8
EXTRA = 128

softmax_scale = 192.0 ** (-0.5)
route_scale = 2.5
norm_eps = 1e-06


def mm(a, b):
    return jnp.dot(a, b, preferred_element_type=F32)


def attend(q, qr, lat, kr, position, length):
    scores = lax.dot_general(q, lat, (((1,), (1,)), ((), ())), preferred_element_type=F32)
    scores = (scores + mm(qr, kr)) * softmax_scale
    key = lax.broadcasted_iota(jnp.int32, scores.shape, 1)
    visible = (key <= position) & (key < length)
    highest = jnp.max(jnp.where(visible, scores, -jnp.inf), axis=1, keepdims=True)
    weights = jnp.where(visible, jnp.exp(scores - highest), 0.0)
    totals = jnp.sum(weights, axis=1, keepdims=True)
    mixed = mm(weights.astype(BF), lat) / totals
    return jnp.where(position[:, :1] < length, mixed, 0.0).astype(BF)


def kernel(
    lengths_s, plan_s,
    qc_h, qr_h, lat_h, kr_h, vu_h, op_h, gain_h, router_h, gu_h, dn_h, routes_h,
    out,
    qc, qr, lat, kr, vu, op, gain, router, gu, dn, rt,
    vals, mv, own, px_send, px_recv, rs_send, rs_recv, mixed,
    a_send, x, gate, upper, logit, square, hid,
    o_own, ox_send, ox_recv, os_send, os_recv, b_send, b_recv, f_send, f_recv,
    l_sem, q_sem, rt_s, rt_r, mv_s, mv_r, px_s, px_r, rs_s, rs_r, a_s, a_r, g_s, g_r, h_s, h_r,
    ox_s, ox_r, os_s, os_r, b_s, b_r, f_s, f_r,
):
    r = lax.axis_index("dp")
    ep = lax.axis_index("ep")
    z = ep // 2
    c = ep % 2
    sib = z * 2 + 1 - c

    def remote(src, dst, ssem, rsem, dp_to, ep_to):
        return pltpu.make_async_remote_copy(
            src_ref=src, dst_ref=dst, send_sem=ssem, recv_sem=rsem,
            device_id=(dp_to, ep_to), device_id_type=MESH)

    loads = [
        (lat_h, lat), (kr_h, kr), (vu_h, vu), (op_h, op), (routes_h, rt.at[z]),
        (gain_h, gain), (router_h, router), (gu_h.at[0], gu), (dn_h.at[0], dn),
    ]
    load = [pltpu.make_async_copy(s, d, l_sem.at[i]) for i, (s, d) in enumerate(loads)]
    qload = []
    for b in range(8):
        to = (b % 2) * HALF + (b // 2) * SPAN
        qload.append(pltpu.make_async_copy(
            qc_h.at[pl.ds(b * SPAN, SPAN)], qc.at[pl.ds(to, SPAN)], q_sem.at[b]))
        qload.append(pltpu.make_async_copy(
            qr_h.at[pl.ds(b * SPAN, SPAN)], qr.at[pl.ds(to, SPAN)], q_sem.at[8 + b]))
    load[0].start()
    load[1].start()
    for cp in reversed(qload):
        cp.start()
    for i in (2, 4, 3, 5, 6, 7, 8):
        load[i].start()

    barrier = pltpu.get_barrier_semaphore()

    def greet(i, carry):
        pl.semaphore_signal(barrier, inc=1, device_id=(lax.rem(r + i, N_DP), ep), device_id_type=MESH)
        return carry

    lax.fori_loop(1, N_DP, greet, 0)
    pl.semaphore_signal(barrier, inc=1, device_id=(r, sib), device_id_type=MESH)
    for dz in (1, 2, 3):
        pl.semaphore_signal(
            barrier, inc=1, device_id=(r, lax.rem(z + dz, N_Z) * 2 + c), device_id_type=MESH)
    pl.semaphore_wait(barrier, N_DP - 1 + 1 + 3)

    load[4].wait()
    for dz in (1, 2, 3):
        remote(rt.at[z], rt.at[z], rt_s.at[dz], rt_r.at[z], r, lax.rem(z + dz, N_Z) * 2 + c).start()

    length = lengths_s[r]
    load[0].wait()
    load[1].wait()
    qload[14].wait()
    qload[15].wait()
    latv = lat[...]
    krv = kr[...]
    q_last = jnp.concatenate(
        [qc[S - SPAN:, h * LAT:(h + 1) * LAT] for h in range(HEADS_HERE)], axis=0)
    r_last = jnp.concatenate(
        [qr[S - SPAN:, h * ROPE:(h + 1) * ROPE] for h in range(HEADS_HERE)], axis=0)
    place = lax.broadcasted_iota(jnp.int32, (HEADS_HERE * SPAN, S), 0)
    att = attend(q_last, r_last, latv, krv, S - SPAN + place % SPAN, length)
    load[2].wait()
    for h in range(HEADS_HERE):
        mv[r, :, h * VDIM:(h + 1) * VDIM] = mm(att[h * SPAN:(h + 1) * SPAN], vu[h]).astype(BF)

    def mv_copy(i):
        to = lax.rem(r + i, N_DP)
        return remote(mv.at[r], mv.at[r], mv_s.at[i], mv_r.at[r], to, ep)

    def mv_start(i, carry):
        mv_copy(i).start()
        return carry

    lax.fori_loop(1, N_DP, mv_start, 0)

    for i in range(14):
        qload[i].wait()
    rows = S - SPAN
    place = lax.broadcasted_iota(jnp.int32, (rows, S), 0)
    position = ((place % HALF) // SPAN * 2 + place // HALF) * SPAN + place % SPAN
    for h in range(HEADS_HERE):
        att = attend(
            qc[:rows, h * LAT:(h + 1) * LAT], qr[:rows, h * ROPE:(h + 1) * ROPE],
            latv, krv, position, length)
        vals[:rows, h * VDIM:(h + 1) * VDIM] = mm(att, vu[h]).astype(BF)

    for dz in (1, 2, 3):
        zz = lax.rem(z + dz, N_Z)
        remote(rt.at[zz], rt.at[zz], rt_s.at[dz], rt_r.at[zz], r, zz * 2 + c).wait_recv()
    first = jnp.concatenate([rt[i, 0:1, :] for i in range(N_Z)], axis=1)
    second = jnp.concatenate([rt[i, 1:2, :] for i in range(N_Z)], axis=1)
    slot = lax.broadcasted_iota(jnp.int32, (N_DP * SLOTS, HALF), 0)
    row = lax.broadcasted_iota(jnp.int32, (N_DP * SLOTS, HALF), 1)
    expert = slot // SLOTS
    named = jnp.where((first == expert) | (second == expert), 1.0, 0.0)
    t_row = lax.broadcasted_iota(jnp.int32, (HALF, HALF), 0)
    t_col = lax.broadcasted_iota(jnp.int32, (HALF, HALF), 1)
    earlier = jnp.where((t_row // SPAN == t_col // SPAN) & (t_row < t_col), 1.0, 0.0).astype(BF)
    before = mm(named.astype(BF), earlier)
    same = (slot // 2) % N_Z == row // SPAN
    chosen_slot = jnp.where(same & (before == (slot % 2).astype(F32)), named, 0.0)
    slots_t = chosen_slot.astype(BF)
    slots = chosen_slot.T.astype(BF)

    def mv_wait(i, carry):
        frm = lax.rem(r + i, N_DP)
        remote(mv.at[frm], mv.at[frm], mv_s.at[i], mv_r.at[frm], frm, ep).wait_recv()
        return carry

    lax.fori_loop(1, N_DP, mv_wait, 0)
    vals[rows:, :] = mv[plan_s[r]]

    load[3].wait()
    order = (2, 1, 3, 0)

    def px_copy(zz):
        return remote(px_send.at[zz], px_recv.at[zz], px_s.at[zz], px_r.at[zz], r, sib)

    def rs_copy(dz, zz):
        return remote(rs_send.at[zz], rs_recv.at[z], rs_s.at[dz], rs_r.at[z], r, zz * 2 + c)

    def pair_sum(dz):
        zz = lax.rem(z + dz, N_Z)
        px_copy(zz).wait_recv()
        total = own[zz] + px_recv[zz].astype(F32)
        if dz:
            rs_send[zz] = total.astype(BF)
            rs_copy(dz, zz).start()
        else:
            mixed[...] = total

    valv = vals[...]
    for n, dz in enumerate(order):
        zz = lax.rem(z + dz, N_Z)
        block = mm(valv, op[:, pl.ds(pl.multiple_of(zz * COLS, 128), COLS)])
        top, bottom = block[:HALF], block[HALF:]
        own[zz] = jnp.where(c == 0, top, bottom)
        px_send[zz] = jnp.where(c == 0, bottom, top).astype(BF)
        px_copy(zz).start()
        if n:
            pair_sum(order[n - 1])
    pair_sum(order[-1])
    total = mixed[...]
    for dz in (1, 3, 2):
        zz = lax.rem(z + dz, N_Z)
        remote(rs_send.at[zz], rs_recv.at[zz], rs_s.at[dz], rs_r.at[zz], r, zz * 2 + c).wait_recv()
        total = total + rs_recv[zz].astype(F32)
    mixed[...] = total

    a_send[...] = mm(slots_t, total.astype(BF)).reshape(N_DP, SLOTS, COLS).astype(BF)

    def a_start(i, carry):
        to = lax.rem(r + i, N_DP)
        remote(a_send.at[to], x.at[z, c, r], a_s.at[i], a_r.at[r], to, ep).start()
        return carry

    lax.fori_loop(1, N_DP, a_start, 0)
    x[z, c, r] = a_send[r]

    def a_wait(i, carry):
        frm = lax.rem(r + i, N_DP)
        remote(a_send.at[frm], x.at[z, c, frm], a_s.at[i], a_r.at[frm], frm, ep).wait_recv()
        return carry

    lax.fori_loop(1, N_DP, a_wait, 0)

    def g_copy(dz, zz, slot):
        return remote(x.at[slot, c], x.at[slot, c], g_s.at[dz], g_r.at[slot], r, zz * 2 + c)

    def h_copy(zz, cc):
        return remote(x.at[zz, cc], x.at[zz, cc], h_s.at[zz], h_r.at[zz], r, sib)

    for dz in (2, 1, 3):
        g_copy(dz, lax.rem(z + dz, N_Z), z).start()
    h_copy(z, c).start()

    for i in (5, 6, 7, 8):
        load[i].wait()
    square[...] = jnp.zeros_like(square)
    gate[...] = jnp.zeros_like(gate)
    upper[...] = jnp.zeros_like(upper)
    logit[...] = jnp.zeros_like(logit)

    def expert_chunk(zz):
        at = pl.multiple_of(zz * COLS, 128)
        m = x[zz].astype(F32).reshape(2 * N_DP * SLOTS, COLS)
        square[...] += jnp.sum(m * m, axis=1, keepdims=True)
        xin = (m * gain[:, pl.ds(at, COLS)]).astype(BF)
        gate[...] += mm(xin, gu[0, pl.ds(at, COLS)])
        upper[...] += mm(xin, gu[1, pl.ds(at, COLS)])
        logit[...] += lax.dot_general(
            xin, router[:, pl.ds(at, COLS)], (((1,), (1,)), ((), ())), preferred_element_type=F32)

    previous = z
    for dz in (1, 3, 2):
        zz = lax.rem(z + dz, N_Z)
        h_copy(previous, 1 - c).wait_recv()
        expert_chunk(previous)
        g_copy(dz, zz, zz).wait_recv()
        h_copy(zz, c).start()
        previous = zz
    h_copy(previous, 1 - c).wait_recv()
    expert_chunk(previous)

    scale = lax.rsqrt(square[...] * (1.0 / D) + norm_eps)
    hid[...] = (jax.nn.silu(gate[...] * scale) * (upper[...] * scale)).astype(BF)
    pick = lax.broadcasted_iota(jnp.int32, logit.shape, 1) == r
    chosen = jax.nn.sigmoid(jnp.sum(jnp.where(pick, logit[...], 0.0), axis=1, keepdims=True) * scale)

    half = N_DP * SLOTS

    def ox_copy(zz):
        return remote(ox_send.at[zz], ox_recv.at[zz], ox_s.at[zz], ox_r.at[zz], r, sib)

    def out_sum(dz):
        zz = lax.rem(z + dz, N_Z)
        ox_copy(zz).wait_recv()
        total = o_own[zz] + ox_recv[zz].astype(F32)
        if dz:
            os_send[zz] = total.astype(BF)
            remote(os_send.at[zz], os_recv.at[z], os_s.at[dz], os_r.at[z], r, zz * 2 + c).start()
        return total

    hidv = hid[...]
    for n, dz in enumerate(order):
        zz = lax.rem(z + dz, N_Z)
        block = mm(hidv, dn[:, pl.ds(pl.multiple_of(zz * COLS, 128), COLS)]) * chosen
        top, bottom = block[:half], block[half:]
        o_own[zz] = jnp.where(c == 0, top, bottom)
        ox_send[zz] = jnp.where(c == 0, bottom, top).astype(BF)
        ox_copy(zz).start()
        if n:
            out_sum(order[n - 1])
    total = out_sum(order[-1])
    for dz in (1, 3, 2):
        zz = lax.rem(z + dz, N_Z)
        remote(os_send.at[zz], os_recv.at[zz], os_s.at[dz], os_r.at[zz], r, zz * 2 + c).wait_recv()
        total = total + os_recv[zz].astype(F32)

    b_send[:, :, :COLS] = total.reshape(N_DP, SLOTS, COLS).astype(BF)
    mine = jnp.where(c == 0, chosen[:half], chosen[half:])
    high = mine.astype(BF).astype(F32)
    low = mine - high
    column = lax.broadcasted_iota(jnp.int32, (half, EXTRA), 1)
    tail = jnp.where(column == 0, high, jnp.where(column == 1, low, 0.0))
    b_send[:, :, COLS:] = tail.reshape(N_DP, SLOTS, EXTRA).astype(BF)

    def b_start(i, carry):
        to = lax.rem(r + i, N_DP)
        remote(b_send.at[to], b_recv.at[r], b_s.at[i], b_r.at[r], to, ep).start()
        return carry

    lax.fori_loop(1, N_DP, b_start, 0)
    b_recv[r] = b_send[r]

    def b_wait(i, carry):
        frm = lax.rem(r + i, N_DP)
        remote(b_send.at[frm], b_recv.at[frm], b_s.at[i], b_r.at[frm], frm, ep).wait_recv()
        return carry

    lax.fori_loop(1, N_DP, b_wait, 0)
    back = b_recv[...].astype(F32).reshape(half, COLS + EXTRA).astype(BF)
    joined = mm(slots, back)
    total_chosen = joined[:, COLS:COLS + 1] + joined[:, COLS + 1:COLS + 2]
    final = mixed[...] + joined[:, :COLS] * (route_scale / total_chosen)
    f_send[...] = final.reshape(N_Z, SPAN, COLS).astype(BF)
    for dz in (2, 1, 3):
        zz = lax.rem(z + dz, N_Z)
        remote(f_send.at[zz], f_recv.at[z], f_s.at[dz], f_r.at[z], r, zz * 2 + c).start()
    f_recv[z] = f_send[z]
    for dz in (1, 3, 2):
        zz = lax.rem(z + dz, N_Z)
        remote(f_send.at[zz], f_recv.at[zz], f_s.at[dz], f_r.at[zz], r, zz * 2 + c).wait_recv()
    for i in range(N_Z):
        out[:, i * COLS:(i + 1) * COLS] = f_recv[i]

    def drain(i, carry):
        to = lax.rem(r + i, N_DP)
        mv_copy(i).wait_send()
        remote(a_send.at[to], x.at[z, c, r], a_s.at[i], a_r.at[r], to, ep).wait_send()
        remote(b_send.at[to], b_recv.at[r], b_s.at[i], b_r.at[r], to, ep).wait_send()
        return carry

    lax.fori_loop(1, N_DP, drain, 0)
    for dz in (0, 1, 2, 3):
        zz = lax.rem(z + dz, N_Z)
        to = zz * 2 + c
        px_copy(zz).wait_send()
        ox_copy(zz).wait_send()
        h_copy(zz, c).wait_send()
        if dz:
            remote(rt.at[z], rt.at[z], rt_s.at[dz], rt_r.at[z], r, to).wait_send()
            rs_copy(dz, zz).wait_send()
            g_copy(dz, zz, z).wait_send()
            remote(os_send.at[zz], os_recv.at[z], os_s.at[dz], os_r.at[z], r, to).wait_send()
            remote(f_send.at[zz], f_recv.at[z], f_s.at[dz], f_r.at[z], r, to).wait_send()


def per_device(
    queries_c, queries_r, latents, key_rope, value_up, out_proj, norm_gain, router, gate_up, down,
    routes, lengths, plan,
):
    any_spec = pl.BlockSpec(memory_space=pl.ANY)
    smem = pl.BlockSpec(memory_space=pltpu.SMEM)
    vm = pltpu.VMEM
    dma = pltpu.SemaphoreType.DMA
    half = N_DP * SLOTS
    scratch = [
        vm((S, HEADS_HERE * LAT), BF), vm((S, HEADS_HERE * ROPE), BF), vm((S, LAT), BF), vm((ROPE, S), BF),
        vm((HEADS_HERE, LAT, VDIM), BF), vm((HEADS_HERE * VDIM, D), BF), vm((1, D), F32),
        vm((N_DP, D), BF), vm((2, D, 256), BF), vm((256, D), BF), vm((N_Z, 2, SPAN), jnp.int32),
        vm((S, HEADS_HERE * VDIM), BF), vm((N_DP, SPAN, HEADS_HERE * VDIM), BF),
        vm((N_Z, HALF, COLS), F32), vm((N_Z, HALF, COLS), BF), vm((N_Z, HALF, COLS), BF),
        vm((N_Z, HALF, COLS), BF), vm((N_Z, HALF, COLS), BF), vm((HALF, COLS), F32),
        vm((N_DP, SLOTS, COLS), BF), vm((N_Z, 2, N_DP, SLOTS, COLS), BF),
        vm((2 * half, 256), F32), vm((2 * half, 256), F32), vm((2 * half, N_DP), F32), vm((2 * half, 1), F32),
        vm((2 * half, 256), BF),
        vm((N_Z, half, COLS), F32), vm((N_Z, half, COLS), BF), vm((N_Z, half, COLS), BF),
        vm((N_Z, half, COLS), BF), vm((N_Z, half, COLS), BF),
        vm((N_DP, SLOTS, COLS + EXTRA), BF), vm((N_DP, SLOTS, COLS + EXTRA), BF),
        vm((N_Z, SPAN, COLS), BF), vm((N_Z, SPAN, COLS), BF),
        dma((9,)), dma((16,)), dma((4,)), dma((4,)), dma((16,)), dma((16,)), dma((4,)), dma((4,)),
        dma((4,)), dma((4,)), dma((16,)), dma((16,)), dma((4,)), dma((4,)), dma((4,)), dma((4,)),
        dma((4,)), dma((4,)), dma((4,)), dma((4,)), dma((16,)), dma((16,)), dma((4,)), dma((4,)),
    ]
    return pl.pallas_call(
        kernel,
        out_shape=jax.ShapeDtypeStruct((SPAN, D), BF),
        in_specs=[smem, smem] + [any_spec] * 11,
        out_specs=pl.BlockSpec(memory_space=pltpu.VMEM),
        scratch_shapes=scratch,
        compiler_params=pltpu.CompilerParams(
            collective_id=0, has_side_effects=True, vmem_limit_bytes=56 * 1024 * 1024),
        cost_estimate=pl.CostEstimate(flops=3 * 10**9, bytes_accessed=16 * 10**6, transcendentals=10**6),
    )(
        lengths, plan, queries_c, queries_r, latents, key_rope, value_up, out_proj,
        norm_gain.reshape(1, D), router.T, gate_up, down, routes.T,
    )


def solution(mesh):
    placed = (
        P("dp", "ep"),
        P("dp", "ep"),
        P("dp", None),
        P(None, "dp"),
        P("ep", None, None),
        P("ep", None),
        P(),
        P(),
        P("dp", None, None, "ep"),
        P("dp", "ep", None),
        P(("dp", "ep"), None),
        P(),
        P(),
    )
    return jax.shard_map(
        per_device, mesh=mesh, in_specs=placed, out_specs=P(("dp", "ep"), None), check_vma=False
    )
```

time: 246 us -> 79.8 us (0.32)
  waiting for transfers between devices: 109 us -> 0 us
  Pallas kernels: 0 us -> 75.7 us
  blocking collectives: 37.5 us -> 0 us
  starting transfers between devices: 28.4 us -> 0 us
  matrix products: 20.7 us -> 0 us
  local copies, waits for them, and re-layouts: 18.7 us -> 2.88 us
  between operations: 15.8 us -> 0.01 us
  other arithmetic: 15.3 us -> 0 us
    all_to_all x5 -> x0, waiting for transfers between devices: 75.8 us -> none  [the longest x1 25.8 us: per_device(): lax.all_to_all(partial_value, ('dp', 'ep'), split_axis=0, concat_axis=0,...]
    pallas_call x0 -> x1, Pallas kernels: none -> 75.7 us  [per_device(): pl.pallas_call(kernel, out_shape=jax.ShapeDtypeStruct((SPAN, D), BF), in_...]
    all_to_all x1 -> x0, blocking collectives: 37.5 us -> none  [per_device(): lax.all_to_all(copies, ('dp', 'ep'), split_axis=0, concat_axis=0, tiled=T...]
    reduce_scatter x1 -> x0, waiting for transfers between devices: 32.8 us -> none  [per_device(): lax.psum_scatter(jnp.dot(values, out_proj, preferred_element_type=jnp.flo...]
    all_to_all x5 -> x0, starting transfers between devices: 28.4 us -> none  [the longest x1 7.58 us: per_device(): lax.all_to_all(slot_out(queries_r[keep_rows:], picked), 'dp', split_axis=...]
    dot_general x12 -> x0, matrix products: 20.7 us -> none  [the longest x1 5.39 us: expert_apply(): return jnp.dot(hidden, down[0], preferred_element_type=jnp.float32)]
    reshape x5 -> x1, local copies, waits for them, and re-layouts: 10.2 us -> 1.33 us  [per_device(): norm_gain.reshape(1, D)]
    reduce_sum x6 -> x0, other arithmetic: 5.92 us -> none  [the longest x1 3.33 us: per_device(): jnp.sum(returned.reshape(rank_count, shard_count, capacity, width).astype...]
  transfers between devices with their start and end apart: 6 -> 0, of which waited for: 6 -> 0; matrix products, arithmetic and copies ran while one was open for 6% -> 0% of each run, Pallas kernels for 0% -> 0%
where the time goes in v1:
time: 79.8 us; the launch traced here: 78.6 us
  Pallas kernels  75.7 us (95%)
  local copies, waits for them, and re-layouts  2.88 us (4%)
    pallas_call x1, Pallas kernels, per_device(): pl.pallas_call(kernel, out_shape=jax.ShapeDtypeStruct((SPAN, D), BF), in_...  75.7 us

profile of v1, /device:TPU:1, one launch (start us, length us, event | category | flops | bytes accessed | tf_op | source)
XLA Modules:
  0.0 78.6 jit_solution(3738137602850546473)
XLA Ops:
  0.0 1.3 %reshape.3.gain_h = f32[1,3584]{1,0:T(1,128)} reshape(f32[3584]{0:T(1024)} %param.19) | data formatting | bytes 28672 | tf_op jit(solution)/shard_map/reshape | solution.py:393
  1.3 75.7 %shard_map.127 = bf16[16,3584]{1,0:T(8,128)(2,1)} custom-call(s32[16]{0:T(128)} %lengths_s.1, s32[16]{0:T(128)} %plan_s.1, bf16[128,4096]{1,0:T(8,128)(2,1)} %qc_h.1, bf16[128,512]{1,0:T(8,128)(2,1)} %qr_h.1, bf16[128,512]{1,0:T(8,128)(2,1)} %lat_h.1, bf16[64,128]{1,0:T(8,128)(2,1)} %kr_h.1, bf16[8,512,128]{2,1,0:T(8,128)(2,1)} %vu_h.1, ...), custom_call_target="tpu_custom_call" | custom-call | flops 3000000000 | bytes 16000000 | tf_op jit(solution)/shard_map/pallas_call | solution.py:382
  77.1 1.6 %copy.15 = bf16[16,3584]{1,0:T(8,128)(2,1)} copy(bf16[16,3584]{1,0:T(8,128)(2,1)} %shard_map.127) | data formatting | bytes 229376

commit v2 on v1

v2 whole, which is shorter than its diff:
```python
import jax
import jax.numpy as jnp
from jax import lax
from jax.experimental import pallas as pl
from jax.experimental.pallas import tpu as pltpu
from jax.sharding import PartitionSpec as P

MESH = pl.DeviceIdType.MESH
BF = jnp.bfloat16
F32 = jnp.float32

D = 3584
LAT = 512
ROPE = 64
VDIM = 128
S = 128
SPAN = 16
HEADS_HERE = 8
N_DP = 16
N_Z = 4
HALF = 64
COLS = D // N_Z
SLOTS = 8
EXTRA = 128

softmax_scale = 192.0 ** (-0.5)
route_scale = 2.5
norm_eps = 1e-06


def mm(a, b):
    return jnp.dot(a, b, preferred_element_type=F32)


def attend(q, qr, lat, kr, position, length):
    scores = lax.dot_general(q, lat, (((1,), (1,)), ((), ())), preferred_element_type=F32)
    scores = (scores + mm(qr, kr)) * softmax_scale
    key = lax.broadcasted_iota(jnp.int32, scores.shape, 1)
    visible = (key <= position) & (key < length)
    highest = jnp.max(jnp.where(visible, scores, -jnp.inf), axis=1, keepdims=True)
    weights = jnp.where(visible, jnp.exp(scores - highest), 0.0)
    totals = jnp.sum(weights, axis=1, keepdims=True)
    mixed = mm(weights.astype(BF), lat) / totals
    return jnp.where(position[:, :1] < length, mixed, 0.0).astype(BF)


def kernel(
    lengths_s, plan_s,
    qc_h, qr_h, lat_h, kr_h, vu_h, op_h, gain_h, router_h, gu_h, dn_h, routes_h,
    out,
    qc, qr, lat, kr, vu, op, gain, router, gu, dn, rt, rt_all,
    vals, own, px_send, px_recv, rs_send, rs_recv, mixed, mv,
    a_send, x, gate, upper, logit, square, hid,
    o_own, ox_send, ox_recv, b_send, b_recv, t_send, t_recv, f_send, f_recv,
    l_sem, q_sem, in_sem, rt_s, rt_r, ra_s, ra_r, mv_s, mv_r, px_s, px_r, rs_s, rs_r, a_s, a_r, h_s, h_r,
    ox_s, ox_r, b_s, b_r, t_s, t_r, f_s, f_r,
):
    r = lax.axis_index("dp")
    ep = lax.axis_index("ep")
    z = ep // 2
    c = ep % 2
    sib = z * 2 + 1 - c

    def remote(src, dst, ssem, rsem, dp_to, ep_to):
        return pltpu.make_async_remote_copy(
            src_ref=src, dst_ref=dst, send_sem=ssem, recv_sem=rsem,
            device_id=(dp_to, ep_to), device_id_type=MESH)

    def peer(dz):
        zz = lax.rem(z + dz, N_Z)
        return zz, zz * 2 + c

    loads = [
        (lat_h, lat), (kr_h, kr), (vu_h, vu), (op_h, op), (routes_h, rt_all.at[r]),
        (gain_h, gain), (router_h, router), (gu_h.at[0], gu), (dn_h.at[0], dn),
    ]
    load = [pltpu.make_async_copy(s, d, l_sem.at[i]) for i, (s, d) in enumerate(loads)]
    qload = []
    for b in range(8):
        to = (b % 2) * HALF + (b // 2) * SPAN
        qload.append(pltpu.make_async_copy(
            qc_h.at[pl.ds(b * SPAN, SPAN)], qc.at[pl.ds(to, SPAN)], q_sem.at[b]))
        qload.append(pltpu.make_async_copy(
            qr_h.at[pl.ds(b * SPAN, SPAN)], qr.at[pl.ds(to, SPAN)], q_sem.at[8 + b]))
    load[0].start()
    load[1].start()
    for cp in qload:
        cp.start()
    for i in (2, 4, 3, 5, 6, 7, 8):
        load[i].start()

    barrier = pltpu.get_barrier_semaphore()

    def greet(i, carry):
        pl.semaphore_signal(barrier, inc=1, device_id=(lax.rem(r + i, N_DP), ep), device_id_type=MESH)
        return carry

    lax.fori_loop(1, N_DP, greet, 0)
    pl.semaphore_signal(barrier, inc=1, device_id=(r, sib), device_id_type=MESH)
    for dz in (1, 2, 3):
        pl.semaphore_signal(barrier, inc=1, device_id=(r, peer(dz)[1]), device_id_type=MESH)

    length = lengths_s[r]
    load[0].wait()
    load[1].wait()
    for cp in qload:
        cp.wait()
    latv = lat[...]
    krv = kr[...]
    place = lax.broadcasted_iota(jnp.int32, (S, S), 0)
    position = ((place % HALF) // SPAN * 2 + place // HALF) * SPAN + place % SPAN
    load[2].wait()
    for h in range(HEADS_HERE):
        att = attend(
            qc[:, h * LAT:(h + 1) * LAT], qr[:, h * ROPE:(h + 1) * ROPE], latv, krv, position, length)
        vals[:, h * VDIM:(h + 1) * VDIM] = mm(att, vu[h]).astype(BF)

    pl.semaphore_wait(barrier, N_DP - 1 + 1 + 3)
    for dz in (1, 2, 3):
        pl.semaphore_signal(in_sem, inc=1, device_id=(r, peer(dz)[1]), device_id_type=MESH)

    load[4].wait()
    last = ep == 2 * N_Z - 1

    @pl.when(last)
    def _():
        def ra_start(i, carry):
            to = lax.rem(r + i, N_DP)
            remote(rt_all.at[r], rt_all.at[r], ra_s.at[i], ra_r.at[r], to, ep).start()
            return carry

        lax.fori_loop(1, N_DP, ra_start, 0)

    load[3].wait()
    order = (2, 1, 3, 0)

    def px_copy(zz):
        return remote(px_send.at[zz], px_recv.at[zz], px_s.at[zz], px_r.at[zz], r, sib)

    def rs_copy(dz):
        zz, to = peer(dz)
        return remote(rs_send.at[zz], rs_recv.at[z], rs_s.at[dz], rs_r.at[z], r, to)

    def pair_sum(dz):
        zz, _ = peer(dz)
        px_copy(zz).wait_recv()
        total = own[zz] + px_recv[zz].astype(F32)
        if dz:
            rs_send[zz] = total.astype(BF)
            rs_copy(dz).start()
        else:
            mixed[...] = total

    valv = vals[...]
    for n, dz in enumerate(order):
        zz, _ = peer(dz)
        block = mm(valv, op[:, pl.ds(pl.multiple_of(zz * COLS, 128), COLS)])
        top, bottom = block[:HALF], block[HALF:]
        own[zz] = jnp.where(c == 0, top, bottom)
        px_send[zz] = jnp.where(c == 0, bottom, top).astype(BF)
        px_copy(zz).start()
        if n:
            pair_sum(order[n - 1])
    pair_sum(order[-1])

    @pl.when(last)
    def _():
        def ra_wait(i, carry):
            frm = lax.rem(r + i, N_DP)
            remote(rt_all.at[frm], rt_all.at[frm], ra_s.at[i], ra_r.at[frm], frm, ep).wait_recv()
            return carry

        lax.fori_loop(1, N_DP, ra_wait, 0)
        rt[z, 0] = rt_all[plan_s[r]]

    @pl.when(jnp.logical_not(last))
    def _():
        rt[z, 0] = rt_all[r]

    rt[z, 1] = rt_all[r]

    def rt_copy(dz, slot):
        return remote(rt.at[slot], rt.at[slot], rt_s.at[dz], rt_r.at[slot], r, peer(dz)[1])

    for dz in (1, 2, 3):
        rt_copy(dz, z).start()
    for dz in (1, 2, 3):
        rt_copy(dz, peer(dz)[0]).wait_recv()
    slot = lax.broadcasted_iota(jnp.int32, (N_DP * SLOTS, HALF), 0)
    row = lax.broadcasted_iota(jnp.int32, (N_DP * SLOTS, HALF), 1)
    expert = slot // SLOTS
    t_row = lax.broadcasted_iota(jnp.int32, (HALF, HALF), 0)
    t_col = lax.broadcasted_iota(jnp.int32, (HALF, HALF), 1)
    earlier = jnp.where((t_row // SPAN == t_col // SPAN) & (t_row < t_col), 1.0, 0.0).astype(BF)
    same = (slot // 2) % N_Z == row // SPAN

    def slot_matrix(which):
        first = jnp.concatenate([rt[i, which, 0:1, :] for i in range(N_Z)], axis=1)
        second = jnp.concatenate([rt[i, which, 1:2, :] for i in range(N_Z)], axis=1)
        named = jnp.where((first == expert) | (second == expert), 1.0, 0.0)
        before = mm(named.astype(BF), earlier)
        return jnp.where(same & (before == (slot % 2).astype(F32)), named, 0.0)

    slots_t = slot_matrix(0).astype(BF)

    total = mixed[...]
    for dz in (1, 3, 2):
        zz, to = peer(dz)
        remote(rs_send.at[zz], rs_recv.at[zz], rs_s.at[dz], rs_r.at[zz], r, to).wait_recv()
        total = total + rs_recv[zz].astype(F32)
    mixed[...] = total

    a_send[...] = mm(slots_t, total.astype(BF)).reshape(N_DP, SLOTS, COLS).astype(BF)
    pl.semaphore_wait(in_sem, 3)

    def a_copy(to, dz):
        return remote(a_send.at[to], x.at[z, c, r], a_s.at[dz], a_r.at[z], to, peer(dz)[1])

    def a_start(i, carry):
        to = lax.rem(r + i, N_DP)
        for dz in range(N_Z):
            a_copy(to, dz).start()
        return carry

    for dz in (1, 2, 3):
        a_copy(r, dz).start()
    lax.fori_loop(1, N_DP, a_start, 0)
    x[z, c, r] = a_send[r]

    def a_wait(zz, count):
        part = x.at[zz, c, pl.ds(0, count)]
        remote(part, part, a_s.at[0], a_r.at[zz], r, sib).wait_recv()

    def h_copy(zz, cc):
        return remote(x.at[zz, cc], x.at[zz, cc], h_s.at[zz], h_r.at[zz], r, sib)

    for i in (5, 6, 7, 8):
        load[i].wait()
    square[...] = jnp.zeros_like(square)
    gate[...] = jnp.zeros_like(gate)
    upper[...] = jnp.zeros_like(upper)
    logit[...] = jnp.zeros_like(logit)

    def expert_chunk(zz):
        at = pl.multiple_of(zz * COLS, 128)
        m = x[zz].astype(F32).reshape(2 * N_DP * SLOTS, COLS)
        square[...] += jnp.sum(m * m, axis=1, keepdims=True)
        xin = (m * gain[:, pl.ds(at, COLS)]).astype(BF)
        gate[...] += mm(xin, gu[0, pl.ds(at, COLS)])
        upper[...] += mm(xin, gu[1, pl.ds(at, COLS)])
        logit[...] += lax.dot_general(
            xin, router[:, pl.ds(at, COLS)], (((1,), (1,)), ((), ())), preferred_element_type=F32)

    previous = None
    for dz in (0, 1, 3, 2):
        zz, _ = peer(dz)
        a_wait(zz, N_DP if dz else N_DP - 1)
        h_copy(zz, c).start()
        if previous is not None:
            h_copy(previous, 1 - c).wait_recv()
            expert_chunk(previous)
        previous = zz
    h_copy(previous, 1 - c).wait_recv()
    expert_chunk(previous)

    def mv_start(i, carry):
        to = lax.rem(r + i, N_DP)
        remote(mv.at[r], mv.at[r], mv_s.at[0], mv_r.at[0], to, ep).start()
        return carry

    @pl.when(c == 1)
    def _():
        mv[r] = mixed[HALF - SPAN:].astype(BF)
        lax.fori_loop(1, N_DP, mv_start, 0)

    scale = lax.rsqrt(square[...] * (1.0 / D) + norm_eps)
    hidv = (jax.nn.silu(gate[...] * scale) * (upper[...] * scale)).astype(BF)
    pick = lax.broadcasted_iota(jnp.int32, logit.shape, 1) == r
    chosen = jax.nn.sigmoid(jnp.sum(jnp.where(pick, logit[...], 0.0), axis=1, keepdims=True) * scale)

    half = N_DP * SLOTS
    to_row = lax.broadcasted_iota(jnp.int32, (2 * half, 2 * half), 0)
    from_row = lax.broadcasted_iota(jnp.int32, (2 * half, 2 * half), 1)
    rank = (to_row % half) // SLOTS
    partner = jnp.zeros_like(rank)
    for i in range(N_DP):
        partner = jnp.where(rank == i, plan_s[i], partner)
    moves = (to_row >= half) & (to_row % SLOTS >= SLOTS - 2)
    wanted = to_row + jnp.where(moves, (partner - rank) * SLOTS, 0)
    swap = jnp.where(from_row == wanted, 1.0, 0.0).astype(BF)
    hid[...] = mm(swap, hidv).astype(BF)
    column = lax.broadcasted_iota(jnp.int32, (2 * half, EXTRA), 1)
    high = chosen.astype(BF).astype(F32)
    tail = jnp.where(column == 0, high, jnp.where(column == 1, chosen - high, 0.0)).astype(BF)
    tail = mm(swap, tail)
    chosen = tail[:, 0:1] + tail[:, 1:2]
    t_send[...] = jnp.where(c == 0, tail[:half], tail[half:]).reshape(N_DP, SLOTS, EXTRA).astype(BF)

    def t_start(i, carry):
        to = lax.rem(r + i, N_DP)
        remote(t_send.at[to], t_recv.at[r], t_s.at[0], t_r.at[0], to, ep).start()
        return carry

    lax.fori_loop(1, N_DP, t_start, 0)
    t_recv[r] = t_send[r]

    def ox_copy(zz):
        return remote(ox_send.at[zz], ox_recv.at[zz], ox_s.at[zz], ox_r.at[zz], r, sib)

    def out_sum(dz):
        zz, to_ep = peer(dz)
        ox_copy(zz).wait_recv()
        total = o_own[zz] + ox_recv[zz].astype(F32)
        b_send[zz] = total.reshape(N_DP, SLOTS, COLS).astype(BF)

        def b_start(i, carry):
            to = lax.rem(r + i, N_DP)
            remote(b_send.at[zz, to], b_recv.at[z, r], b_s.at[dz], b_r.at[z], to, to_ep).start()
            return carry

        lax.fori_loop(0 if dz else 1, N_DP, b_start, 0)
        if dz == 0:
            b_recv[z, r] = b_send[z, r]

    hidv = hid[...]
    for n, dz in enumerate(order):
        zz, _ = peer(dz)
        block = mm(hidv, dn[:, pl.ds(pl.multiple_of(zz * COLS, 128), COLS)]) * chosen
        top, bottom = block[:half], block[half:]
        o_own[zz] = jnp.where(c == 0, top, bottom)
        ox_send[zz] = jnp.where(c == 0, bottom, top).astype(BF)
        ox_copy(zz).start()
        if n:
            out_sum(order[n - 1])
    out_sum(order[-1])

    def mv_all():
        part = mv.at[pl.ds(0, N_DP - 1)]
        return remote(part, part, mv_s.at[0], mv_r.at[0], r, sib)

    @pl.when(c == 1)
    def _():
        mv_all().wait_recv()
        mixed[HALF - SPAN:, :] = mv[plan_s[r]].astype(F32)

    slots = slot_matrix(1).T.astype(BF)
    t_part = t_recv.at[pl.ds(0, N_DP - 1)]
    remote(t_part, t_part, t_s.at[0], t_r.at[0], r, sib).wait_recv()
    weight = mm(slots, t_recv[...].astype(F32).reshape(half, EXTRA).astype(BF))
    factor = route_scale / (weight[:, 0:1] + weight[:, 1:2])
    joined = jnp.zeros((HALF, COLS), F32)
    for dz in (0, 1, 3, 2):
        zz, _ = peer(dz)
        part = b_recv.at[zz, pl.ds(0, N_DP if dz else N_DP - 1)]
        remote(part, part, b_s.at[0], b_r.at[zz], r, sib).wait_recv()
        joined = joined + mm(slots, b_recv[zz].astype(F32).reshape(half, COLS).astype(BF))
    final = mixed[...] + joined * factor
    f_send[...] = final.reshape(N_Z, SPAN, COLS).astype(BF)

    def f_copy(dz):
        zz, to = peer(dz)
        return remote(f_send.at[zz], f_recv.at[z], f_s.at[dz], f_r.at[z], r, to)

    for dz in (2, 1, 3):
        f_copy(dz).start()
    f_recv[z] = f_send[z]
    for dz in (1, 3, 2):
        zz, to = peer(dz)
        remote(f_send.at[zz], f_recv.at[zz], f_s.at[dz], f_r.at[zz], r, to).wait_recv()
    for i in range(N_Z):
        out[:, i * COLS:(i + 1) * COLS] = f_recv[i]

    for dz in range(N_Z):
        zz, to = peer(dz)
        count = N_DP if dz else N_DP - 1
        part = b_send.at[zz, pl.ds(0, count)]
        remote(part, part, b_s.at[dz], b_r.at[zz], r, sib).wait_send()
        part = a_send.at[pl.ds(0, count)]
        remote(part, part, a_s.at[dz], a_r.at[zz], r, sib).wait_send()
        px_copy(zz).wait_send()
        ox_copy(zz).wait_send()
        h_copy(zz, c).wait_send()
        if dz:
            rt_copy(dz, z).wait_send()
            rs_copy(dz).wait_send()
            f_copy(dz).wait_send()
    remote(t_part, t_part, t_s.at[0], t_r.at[0], r, sib).wait_send()

    @pl.when(c == 1)
    def _():
        mv_all().wait_send()

    @pl.when(last)
    def _():
        def ra_drain(i, carry):
            to = lax.rem(r + i, N_DP)
            remote(rt_all.at[r], rt_all.at[r], ra_s.at[i], ra_r.at[r], to, ep).wait_send()
            return carry

        lax.fori_loop(1, N_DP, ra_drain, 0)


def per_device(
    queries_c, queries_r, latents, key_rope, value_up, out_proj, norm_gain, router, gate_up, down,
    routes, lengths, plan,
):
    any_spec = pl.BlockSpec(memory_space=pl.ANY)
    smem = pl.BlockSpec(memory_space=pltpu.SMEM)
    vm = pltpu.VMEM
    dma = pltpu.SemaphoreType.DMA
    half = N_DP * SLOTS
    scratch = [
        vm((S, HEADS_HERE * LAT), BF), vm((S, HEADS_HERE * ROPE), BF), vm((S, LAT), BF), vm((ROPE, S), BF),
        vm((HEADS_HERE, LAT, VDIM), BF), vm((HEADS_HERE * VDIM, D), BF), vm((1, D), F32),
        vm((N_DP, D), BF), vm((2, D, 256), BF), vm((256, D), BF),
        vm((N_Z, 2, 2, SPAN), jnp.int32), vm((N_DP, 2, SPAN), jnp.int32),
        vm((S, HEADS_HERE * VDIM), BF),
        vm((N_Z, HALF, COLS), F32), vm((N_Z, HALF, COLS), BF), vm((N_Z, HALF, COLS), BF),
        vm((N_Z, HALF, COLS), BF), vm((N_Z, HALF, COLS), BF), vm((HALF, COLS), F32),
        vm((N_DP, SPAN, COLS), BF),
        vm((N_DP, SLOTS, COLS), BF), vm((N_Z, 2, N_DP, SLOTS, COLS), BF),
        vm((2 * half, 256), F32), vm((2 * half, 256), F32), vm((2 * half, N_DP), F32), vm((2 * half, 1), F32),
        vm((2 * half, 256), BF),
        vm((N_Z, half, COLS), F32), vm((N_Z, half, COLS), BF), vm((N_Z, half, COLS), BF),
        vm((N_Z, N_DP, SLOTS, COLS), BF), vm((N_Z, N_DP, SLOTS, COLS), BF),
        vm((N_DP, SLOTS, EXTRA), BF), vm((N_DP, SLOTS, EXTRA), BF),
        vm((N_Z, SPAN, COLS), BF), vm((N_Z, SPAN, COLS), BF),
        dma((9,)), dma((16,)), pltpu.SemaphoreType.REGULAR, dma((4,)), dma((4,)), dma((16,)), dma((16,)),
        dma((1,)), dma((1,)), dma((4,)), dma((4,)), dma((4,)), dma((4,)), dma((4,)), dma((4,)),
        dma((4,)), dma((4,)), dma((4,)), dma((4,)), dma((4,)), dma((4,)), dma((1,)), dma((1,)),
        dma((4,)), dma((4,)),
    ]
    return pl.pallas_call(
        kernel,
        out_shape=jax.ShapeDtypeStruct((SPAN, D), BF),
        in_specs=[smem, smem] + [any_spec] * 11,
        out_specs=pl.BlockSpec(memory_space=pltpu.VMEM),
        scratch_shapes=scratch,
        compiler_params=pltpu.CompilerParams(
            collective_id=0, has_side_effects=True, vmem_limit_bytes=56 * 1024 * 1024),
        cost_estimate=pl.CostEstimate(flops=3 * 10**9, bytes_accessed=16 * 10**6, transcendentals=10**6),
    )(
        lengths, plan, queries_c, queries_r, latents, key_rope, value_up, out_proj,
        norm_gain.reshape(1, D), router.T, gate_up, down, routes.T,
    )


def solution(mesh):
    placed = (
        P("dp", "ep"),
        P("dp", "ep"),
        P("dp", None),
        P(None, "dp"),
        P("ep", None, None),
        P("ep", None),
        P(),
        P(),
        P("dp", None, None, "ep"),
        P("dp", "ep", None),
        P(("dp", "ep"), None),
        P(),
        P(),
    )
    return jax.shard_map(
        per_device, mesh=mesh, in_specs=placed, out_specs=P(("dp", "ep"), None), check_vma=False
    )
```

time: 79.8 us -> 68.5 us (0.86); the launches traced: 78.6 us -> 68.3 us
  Pallas kernels: 75.7 us -> 65.4 us
    pallas_call x1, Pallas kernels: 75.7 us -> 65.4 us  [per_device(): pl.pallas_call(kernel, out_shape=jax.ShapeDtypeStruct((SPAN, D), BF), in_...]
where the time goes in v2:
time: 68.5 us; the launch traced here: 68.3 us
  Pallas kernels  65.4 us (95%)
  local copies, waits for them, and re-layouts  2.88 us (4%)
    pallas_call x1, Pallas kernels, per_device(): pl.pallas_call(kernel, out_shape=jax.ShapeDtypeStruct((SPAN, D), BF), in_...  65.4 us
    unnamed x1, local copies, waits for them, and re-layouts  1.55 us

profile of v2, /device:TPU:1, one launch (start us, length us, event | category | flops | bytes accessed | tf_op | source)
XLA Modules:
  0.0 68.3 jit_solution(1441274530125132566)
XLA Ops:
  0.0 1.3 %reshape.3.gain_h = f32[1,3584]{1,0:T(1,128)} reshape(f32[3584]{0:T(1024)} %param.19) | data formatting | bytes 28672 | tf_op jit(solution)/shard_map/reshape | solution.py:444
  1.3 65.4 %shard_map.127 = bf16[16,3584]{1,0:T(8,128)(2,1)} custom-call(s32[16]{0:T(128)} %lengths_s.1, s32[16]{0:T(128)} %plan_s.1, bf16[128,4096]{1,0:T(8,128)(2,1)} %qc_h.1, bf16[128,512]{1,0:T(8,128)(2,1)} %qr_h.1, bf16[128,512]{1,0:T(8,128)(2,1)} %lat_h.1, bf16[64,128]{1,0:T(8,128)(2,1)} %kr_h.1, bf16[8,512,128]{2,1,0:T(8,128)(2,1)} %vu_h.1, ...), custom_call_target="tpu_custom_call" | custom-call | flops 3000000000 | bytes 16000000 | tf_op jit(solution)/shard_map/pallas_call | solution.py:433
  66.8 1.6 %copy.15 = bf16[16,3584]{1,0:T(8,128)(2,1)} copy(bf16[16,3584]{1,0:T(8,128)(2,1)} %shard_map.127) | data formatting | bytes 229376

commit v3 on v2

--- a/solution.py
+++ b/solution.py
@@ -45,14 +45,13 @@
 
 
 def kernel(
-    lengths_s, plan_s,
-    qc_h, qr_h, lat_h, kr_h, vu_h, op_h, gain_h, router_h, gu_h, dn_h, routes_h,
+    lengths_h, plan_h, qc_h, qr_h, lat_h, kr_h, vu_h, op_h, gain_h, router_h, gu_h, dn_h, routes_h,
     out,
-    qc, qr, lat, kr, vu, op, gain, router, gu, dn, rt, rt_all,
-    vals, own, px_send, px_recv, rs_send, rs_recv, mixed, mv,
+    lengths_s, plan_s, qc, qr, lat, kr, vu, op, gain, router, gu, dn, rt, rt_all,
+    vals, own, px_send, px_recv, rs_send, rs_recv, mixed,
     a_send, x, gate, upper, logit, square, hid,
-    o_own, ox_send, ox_recv, b_send, b_recv, t_send, t_recv, f_send, f_recv,
-    l_sem, q_sem, in_sem, rt_s, rt_r, ra_s, ra_r, mv_s, mv_r, px_s, px_r, rs_s, rs_r, a_s, a_r, h_s, h_r,
+    o_own, residual, ox_send, ox_recv, b_send, b_recv, t_send, t_recv, f_send, f_recv,
+    l_sem, q_sem, o_sem, in_sem, rt_s, rt_r, ra_s, ra_r, px_s, px_r, rs_s, rs_r, a_s, a_r, h_s, h_r,
     ox_s, ox_r, b_s, b_r, t_s, t_r, f_s, f_r,
 ):
     r = lax.axis_index("dp")
@@ -70,9 +69,20 @@
         zz = lax.rem(z + dz, N_Z)
         return zz, zz * 2 + c
 
+    barrier = pltpu.get_barrier_semaphore()
+
+    def greet(i, carry):
+        pl.semaphore_signal(barrier, inc=1, device_id=(lax.rem(r + i, N_DP), ep), device_id_type=MESH)
+        return carry
+
+    lax.fori_loop(1, N_DP, greet, 0)
+    pl.semaphore_signal(barrier, inc=1, device_id=(r, sib), device_id_type=MESH)
+    for dz in (1, 2, 3):
+        pl.semaphore_signal(barrier, inc=1, device_id=(r, peer(dz)[1]), device_id_type=MESH)
+
     loads = [
         (lat_h, lat), (kr_h, kr), (vu_h, vu), (op_h, op), (routes_h, rt_all.at[r]),
-        (gain_h, gain), (router_h, router), (gu_h.at[0], gu), (dn_h.at[0], dn),
+        (gain_h, gain), (router_h, router), (gu_h.at[0], gu), (dn_h.at[0], dn), (lengths_h, lengths_s), (plan_h, plan_s),
     ]
     load = [pltpu.make_async_copy(s, d, l_sem.at[i]) for i, (s, d) in enumerate(loads)]
     qload = []
@@ -82,29 +92,21 @@
             qc_h.at[pl.ds(b * SPAN, SPAN)], qc.at[pl.ds(to, SPAN)], q_sem.at[b]))
         qload.append(pltpu.make_async_copy(
             qr_h.at[pl.ds(b * SPAN, SPAN)], qr.at[pl.ds(to, SPAN)], q_sem.at[8 + b]))
+    load[9].start()
     load[0].start()
     load[1].start()
     for cp in qload:
         cp.start()
-    for i in (2, 4, 3, 5, 6, 7, 8):
-        load[i].start()
-
-    barrier = pltpu.get_barrier_semaphore()
-
-    def greet(i, carry):
-        pl.semaphore_signal(barrier, inc=1, device_id=(lax.rem(r + i, N_DP), ep), device_id_type=MESH)
-        return carry
-
-    lax.fori_loop(1, N_DP, greet, 0)
-    pl.semaphore_signal(barrier, inc=1, device_id=(r, sib), device_id_type=MESH)
-    for dz in (1, 2, 3):
-        pl.semaphore_signal(barrier, inc=1, device_id=(r, peer(dz)[1]), device_id_type=MESH)
-
-    length = lengths_s[r]
+    load[2].start()
+
     load[0].wait()
     load[1].wait()
     for cp in qload:
         cp.wait()
+    for i in (3, 4, 10, 5, 6, 7, 8):
+        load[i].start()
+    load[9].wait()
+    length = lengths_s[r]
     latv = lat[...]
     krv = kr[...]
     place = lax.broadcasted_iota(jnp.int32, (S, S), 0)
@@ -120,6 +122,7 @@
         pl.semaphore_signal(in_sem, inc=1, device_id=(r, peer(dz)[1]), device_id_type=MESH)
 
     load[4].wait()
+    load[10].wait()
     last = ep == 2 * N_Z - 1
 
     @pl.when(last)
@@ -208,7 +211,6 @@
         zz, to = peer(dz)
         remote(rs_send.at[zz], rs_recv.at[zz], rs_s.at[dz], rs_r.at[zz], r, to).wait_recv()
         total = total + rs_recv[zz].astype(F32)
-    mixed[...] = total
 
     a_send[...] = mm(slots_t, total.astype(BF)).reshape(N_DP, SLOTS, COLS).astype(BF)
     pl.semaphore_wait(in_sem, 3)
@@ -245,7 +247,7 @@
         at = pl.multiple_of(zz * COLS, 128)
         m = x[zz].astype(F32).reshape(2 * N_DP * SLOTS, COLS)
         square[...] += jnp.sum(m * m, axis=1, keepdims=True)
-        xin = (m * gain[:, pl.ds(at, COLS)]).astype(BF)
+        xin = (m * gain[pl.ds(at, COLS)].reshape(1, COLS)).astype(BF)
         gate[...] += mm(xin, gu[0, pl.ds(at, COLS)])
         upper[...] += mm(xin, gu[1, pl.ds(at, COLS)])
         logit[...] += lax.dot_general(
@@ -262,16 +264,6 @@
         previous = zz
     h_copy(previous, 1 - c).wait_recv()
     expert_chunk(previous)
-
-    def mv_start(i, carry):
-        to = lax.rem(r + i, N_DP)
-        remote(mv.at[r], mv.at[r], mv_s.at[0], mv_r.at[0], to, ep).start()
-        return carry
-
-    @pl.when(c == 1)
-    def _():
-        mv[r] = mixed[HALF - SPAN:].astype(BF)
-        lax.fori_loop(1, N_DP, mv_start, 0)
 
     scale = lax.rsqrt(square[...] * (1.0 / D) + norm_eps)
     hidv = (jax.nn.silu(gate[...] * scale) * (upper[...] * scale)).astype(BF)
@@ -304,6 +296,10 @@
     lax.fori_loop(1, N_DP, t_start, 0)
     t_recv[r] = t_send[r]
 
+    swap_half = jnp.where(c == 0, swap[:half, :half], swap[half:, half:])
+    mine = jnp.where(c == 0, chosen[:half], chosen[half:]) * (1.0 / route_scale)
+    residual[...] = mm(swap_half, x[z, c].astype(F32).reshape(half, COLS).astype(BF)) * mine
+
     def ox_copy(zz):
         return remote(ox_send.at[zz], ox_recv.at[zz], ox_s.at[zz], ox_r.at[zz], r, sib)
 
@@ -311,6 +307,8 @@
         zz, to_ep = peer(dz)
         ox_copy(zz).wait_recv()
         total = o_own[zz] + ox_recv[zz].astype(F32)
+        if dz == 0:
+            total = total + residual[...]
         b_send[zz] = total.reshape(N_DP, SLOTS, COLS).astype(BF)
 
         def b_start(i, carry):
@@ -334,15 +332,6 @@
             out_sum(order[n - 1])
     out_sum(order[-1])
 
-    def mv_all():
-        part = mv.at[pl.ds(0, N_DP - 1)]
-        return remote(part, part, mv_s.at[0], mv_r.at[0], r, sib)
-
-    @pl.when(c == 1)
-    def _():
-        mv_all().wait_recv()
-        mixed[HALF - SPAN:, :] = mv[plan_s[r]].astype(F32)
-
     slots = slot_matrix(1).T.astype(BF)
     t_part = t_recv.at[pl.ds(0, N_DP - 1)]
     remote(t_part, t_part, t_s.at[0], t_r.at[0], r, sib).wait_recv()
@@ -354,7 +343,7 @@
         part = b_recv.at[zz, pl.ds(0, N_DP if dz else N_DP - 1)]
         remote(part, part, b_s.at[0], b_r.at[zz], r, sib).wait_recv()
         joined = joined + mm(slots, b_recv[zz].astype(F32).reshape(half, COLS).astype(BF))
-    final = mixed[...] + joined * factor
+    final = joined * factor
     f_send[...] = final.reshape(N_Z, SPAN, COLS).astype(BF)
 
     def f_copy(dz):
@@ -364,12 +353,19 @@
     for dz in (2, 1, 3):
         f_copy(dz).start()
     f_recv[z] = f_send[z]
+
+    def store(zz):
+        columns = pl.ds(pl.multiple_of(zz * COLS, 128), COLS)
+        return pltpu.make_async_copy(f_recv.at[zz], out.at[:, columns], o_sem.at[zz])
+
+    store(z).start()
     for dz in (1, 3, 2):
         zz, to = peer(dz)
         remote(f_send.at[zz], f_recv.at[zz], f_s.at[dz], f_r.at[zz], r, to).wait_recv()
+        store(zz).start()
+
     for i in range(N_Z):
-        out[:, i * COLS:(i + 1) * COLS] = f_recv[i]
-
+        store(i).wait()
     for dz in range(N_Z):
         zz, to = peer(dz)
         count = N_DP if dz else N_DP - 1
@@ -386,10 +382,6 @@
             f_copy(dz).wait_send()
     remote(t_part, t_part, t_s.at[0], t_r.at[0], r, sib).wait_send()
 
-    @pl.when(c == 1)
-    def _():
-        mv_all().wait_send()
-
     @pl.when(last)
     def _():
         def ra_drain(i, carry):
@@ -405,43 +397,42 @@
     routes, lengths, plan,
 ):
     any_spec = pl.BlockSpec(memory_space=pl.ANY)
-    smem = pl.BlockSpec(memory_space=pltpu.SMEM)
     vm = pltpu.VMEM
     dma = pltpu.SemaphoreType.DMA
     half = N_DP * SLOTS
     scratch = [
+        pltpu.SMEM((N_DP,), jnp.int32), pltpu.SMEM((N_DP,), jnp.int32),
         vm((S, HEADS_HERE * LAT), BF), vm((S, HEADS_HERE * ROPE), BF), vm((S, LAT), BF), vm((ROPE, S), BF),
-        vm((HEADS_HERE, LAT, VDIM), BF), vm((HEADS_HERE * VDIM, D), BF), vm((1, D), F32),
+        vm((HEADS_HERE, LAT, VDIM), BF), vm((HEADS_HERE * VDIM, D), BF), vm((D,), F32),
         vm((N_DP, D), BF), vm((2, D, 256), BF), vm((256, D), BF),
         vm((N_Z, 2, 2, SPAN), jnp.int32), vm((N_DP, 2, SPAN), jnp.int32),
         vm((S, HEADS_HERE * VDIM), BF),
         vm((N_Z, HALF, COLS), F32), vm((N_Z, HALF, COLS), BF), vm((N_Z, HALF, COLS), BF),
         vm((N_Z, HALF, COLS), BF), vm((N_Z, HALF, COLS), BF), vm((HALF, COLS), F32),
-        vm((N_DP, SPAN, COLS), BF),
         vm((N_DP, SLOTS, COLS), BF), vm((N_Z, 2, N_DP, SLOTS, COLS), BF),
         vm((2 * half, 256), F32), vm((2 * half, 256), F32), vm((2 * half, N_DP), F32), vm((2 * half, 1), F32),
         vm((2 * half, 256), BF),
-        vm((N_Z, half, COLS), F32), vm((N_Z, half, COLS), BF), vm((N_Z, half, COLS), BF),
+        vm((N_Z, half, COLS), F32), vm((half, COLS), F32), vm((N_Z, half, COLS), BF), vm((N_Z, half, COLS), BF),
         vm((N_Z, N_DP, SLOTS, COLS), BF), vm((N_Z, N_DP, SLOTS, COLS), BF),
         vm((N_DP, SLOTS, EXTRA), BF), vm((N_DP, SLOTS, EXTRA), BF),
         vm((N_Z, SPAN, COLS), BF), vm((N_Z, SPAN, COLS), BF),
-        dma((9,)), dma((16,)), pltpu.SemaphoreType.REGULAR, dma((4,)), dma((4,)), dma((16,)), dma((16,)),
-        dma((1,)), dma((1,)), dma((4,)), dma((4,)), dma((4,)), dma((4,)), dma((4,)), dma((4,)),
+        dma((11,)), dma((16,)), dma((4,)), pltpu.SemaphoreType.REGULAR, dma((4,)), dma((4,)), dma((16,)), dma((16,)),
+        dma((4,)), dma((4,)), dma((4,)), dma((4,)), dma((4,)), dma((4,)),
         dma((4,)), dma((4,)), dma((4,)), dma((4,)), dma((4,)), dma((4,)), dma((1,)), dma((1,)),
         dma((4,)), dma((4,)),
     ]
     return pl.pallas_call(
         kernel,
         out_shape=jax.ShapeDtypeStruct((SPAN, D), BF),
-        in_specs=[smem, smem] + [any_spec] * 11,
-        out_specs=pl.BlockSpec(memory_space=pltpu.VMEM),
+        in_specs=[any_spec] * 13,
+        out_specs=any_spec,
         scratch_shapes=scratch,
         compiler_params=pltpu.CompilerParams(
             collective_id=0, has_side_effects=True, vmem_limit_bytes=56 * 1024 * 1024),
         cost_estimate=pl.CostEstimate(flops=3 * 10**9, bytes_accessed=16 * 10**6, transcendentals=10**6),
     )(
         lengths, plan, queries_c, queries_r, latents, key_rope, value_up, out_proj,
-        norm_gain.reshape(1, D), router.T, gate_up, down, routes.T,
+        norm_gain, router.T, gate_up, down, routes.T,
     )
 
 

time: 68.5 us -> 63.6 us (0.928)
  Pallas kernels: 65.4 us -> 61.9 us
  local copies, waits for them, and re-layouts: 2.88 us -> 1.55 us
    pallas_call x1, Pallas kernels: 65.4 us -> 61.9 us  [per_device(): pl.pallas_call(kernel, out_shape=jax.ShapeDtypeStruct((SPAN, D), BF), in_...]
    reshape x1 -> x0, local copies, waits for them, and re-layouts: 1.33 us -> none  [per_device(): norm_gain.reshape(1, D)]
where the time goes in v3:
time: 63.6 us; the launch traced here: 63.4 us
  Pallas kernels  61.9 us (97%)
  local copies, waits for them, and re-layouts  1.55 us (2%)
    pallas_call x1, Pallas kernels, per_device(): pl.pallas_call(kernel, out_shape=jax.ShapeDtypeStruct((SPAN, D), BF), in_...  61.9 us
    unnamed x1, local copies, waits for them, and re-layouts  1.55 us

profile of v3, /device:TPU:1, one launch (start us, length us, event | category | flops | bytes accessed | tf_op | source)
XLA Modules:
  0.0 63.4 jit_solution(13802796809429410392)
XLA Ops:
  0.0 61.9 %shard_map.127 = bf16[16,3584]{1,0:T(8,128)(2,1)} custom-call(s32[16]{0:T(128)} %lengths_h.1, s32[16]{0:T(128)} %plan_h.1, bf16[128,4096]{1,0:T(8,128)(2,1)} %qc_h.1, bf16[128,512]{1,0:T(8,128)(2,1)} %qr_h.1, bf16[128,512]{1,0:T(8,128)(2,1)} %lat_h.1, bf16[64,128]{1,0:T(8,128)(2,1)} %kr_h.1, bf16[8,512,128]{2,1,0:T(8,128)(2,1)} %vu_h.1, ...), custom_call_target="tpu_custom_call" | custom-call | flops 3000000000 | bytes 16000000 | tf_op jit(solution)/shard_map/pallas_call | solution.py:424
  61.9 1.6 %copy.15 = bf16[16,3584]{1,0:T(8,128)(2,1)} copy(bf16[16,3584]{1,0:T(8,128)(2,1)} %shard_map.127) | data formatting | bytes 229376

commit v4 on v3

v4 whole, which is shorter than its diff:
```python
import jax
import jax.numpy as jnp
from jax import lax
from jax.experimental import pallas as pl
from jax.experimental.pallas import tpu as pltpu
from jax.sharding import PartitionSpec as P

MESH = pl.DeviceIdType.MESH
BF = jnp.bfloat16
F32 = jnp.float32

D = 3584
LAT = 512
ROPE = 64
VDIM = 128
S = 128
SPAN = 16
HEADS_HERE = 8
N_DP = 16
N_Z = 4
HALF = 64
COLS = D // N_Z
SLOTS = 8
EXTRA = 128
LAG = 2
PIECES = ((0, 384), (384, 512))

softmax_scale = 192.0 ** (-0.5)
route_scale = 2.5
norm_eps = 1e-06


def mm(a, b):
    return jnp.dot(a, b, preferred_element_type=F32)


def attend(q, qr, lat, kr, position, length):
    scores = lax.dot_general(q, lat, (((1,), (1,)), ((), ())), preferred_element_type=F32)
    scores = (scores + mm(qr, kr)) * softmax_scale
    key = lax.broadcasted_iota(jnp.int32, scores.shape, 1)
    visible = (key <= position) & (key < length)
    highest = jnp.max(jnp.where(visible, scores, -jnp.inf), axis=1, keepdims=True)
    weights = jnp.where(visible, jnp.exp(scores - highest), 0.0)
    totals = jnp.sum(weights, axis=1, keepdims=True)
    mixed = mm(weights.astype(BF), lat) / totals
    return jnp.where(position[:, :1] < length, mixed, 0.0).astype(BF)


def kernel(
    lengths_h, plan_h, qc_h, qr_h, lat_h, kr_h, vu_h, op_h, gain_h, router_h, gu_h, dn_h, routes_h,
    out,
    lengths_s, plan_s, qc, qr, lat, kr, vu, op, gain, router, gu, dn, rt, rt_all, rt_last,
    vals, gate, upper, logit, square, swap,
    o_own, residual, ox_send, ox_recv, b_send, b_recv, t_send, t_recv, f_send, f_recv, weight, result,
    *rest,
):
    n_pieces = len(PIECES)
    own, px_send, px_recv, rs_send, rs_recv, a_send, x = (
        rest[i * n_pieces:(i + 1) * n_pieces] for i in range(7))
    (l_sem, q_sem, o_sem, in_sem, rt_s, rt_r, ra_s, ra_r, px_s, px_r, rs_s, rs_r, a_s, a_r, h_s, h_r,
     ox_s, ox_r, b_s, b_r, t_s, t_r, f_s, f_r) = rest[7 * n_pieces:]
    r = lax.axis_index("dp")
    ep = lax.axis_index("ep")
    z = ep // 2
    c = ep % 2
    sib = z * 2 + 1 - c

    def remote(src, dst, ssem, rsem, dp_to, ep_to):
        return pltpu.make_async_remote_copy(
            src_ref=src, dst_ref=dst, send_sem=ssem, recv_sem=rsem,
            device_id=(dp_to, ep_to), device_id_type=MESH)

    def peer(dz):
        zz = lax.rem(z + dz, N_Z)
        return zz, zz * 2 + c

    barrier = pltpu.get_barrier_semaphore()

    def greet(i, carry):
        pl.semaphore_signal(barrier, inc=1, device_id=(lax.rem(r + i, N_DP), ep), device_id_type=MESH)
        return carry

    lax.fori_loop(1, N_DP, greet, 0)
    pl.semaphore_signal(barrier, inc=1, device_id=(r, sib), device_id_type=MESH)
    for dz in (1, 2, 3):
        pl.semaphore_signal(barrier, inc=1, device_id=(r, peer(dz)[1]), device_id_type=MESH)

    loads = [
        (lat_h, lat), (kr_h, kr), (vu_h, vu), (op_h, op), (routes_h, rt.at[z]),
        (gain_h, gain), (router_h, router), (gu_h.at[0], gu), (dn_h.at[0], dn), (lengths_h, lengths_s), (plan_h, plan_s),
    ]
    load = [pltpu.make_async_copy(s, d, l_sem.at[i]) for i, (s, d) in enumerate(loads)]
    qload = []
    for b in range(8):
        to = (b % 2) * HALF + (b // 2) * SPAN
        qload.append(pltpu.make_async_copy(
            qc_h.at[pl.ds(b * SPAN, SPAN)], qc.at[pl.ds(to, SPAN)], q_sem.at[b]))
        qload.append(pltpu.make_async_copy(
            qr_h.at[pl.ds(b * SPAN, SPAN)], qr.at[pl.ds(to, SPAN)], q_sem.at[8 + b]))
    for i in (9, 10, 4):
        load[i].start()
    load[0].start()
    load[1].start()
    for cp in qload:
        cp.start()
    load[2].start()

    load[0].wait()
    load[1].wait()
    for cp in qload:
        cp.wait()
    for i in (3, 5, 6, 7, 8):
        load[i].start()
    load[9].wait()
    length = lengths_s[r]
    latv = lat[...]
    krv = kr[...]
    place = lax.broadcasted_iota(jnp.int32, (S, S), 0)
    position = ((place % HALF) // SPAN * 2 + place // HALF) * SPAN + place % SPAN
    load[2].wait()
    for h in range(HEADS_HERE):
        att = attend(
            qc[:, h * LAT:(h + 1) * LAT], qr[:, h * ROPE:(h + 1) * ROPE], latv, krv, position, length)
        vals[:, h * VDIM:(h + 1) * VDIM] = mm(att, vu[h]).astype(BF)

    pl.semaphore_wait(barrier, N_DP - 1 + 1 + 3)
    for dz in (1, 2, 3):
        pl.semaphore_signal(in_sem, inc=1, device_id=(r, peer(dz)[1]), device_id_type=MESH)

    load[4].wait()
    load[10].wait()

    def rt_copy(dz, slot):
        return remote(rt.at[slot], rt.at[slot], rt_s.at[dz], rt_r.at[slot], r, peer(dz)[1])

    for dz in (1, 2, 3):
        rt_copy(dz, z).start()

    load[3].wait()
    order = (2, 1, 3, 0)

    def px_copy(p, zz):
        return remote(px_send[p].at[zz], px_recv[p].at[zz], px_s.at[p, zz], px_r.at[p, zz], r, sib)

    def rs_copy(p, dz):
        zz, to = peer(dz)
        return remote(rs_send[p].at[zz], rs_recv[p].at[z], rs_s.at[p, dz], rs_r.at[p, z], r, to)

    def pair_sum(p, dz):
        zz, _ = peer(dz)
        px_copy(p, zz).wait_recv()
        total = own[p][zz] + px_recv[p][zz].astype(F32)
        if dz:
            rs_send[p][zz] = total.astype(BF)
            rs_copy(p, dz).start()
        else:
            own[p][zz] = total

    def ra_all():
        part = rt_all.at[pl.ds(0, N_DP - 1)]
        return remote(part, part, ra_s.at[0], ra_r.at[0], r, sib)

    def spread_routes():
        for dz in (1, 2, 3):
            rt_copy(dz, peer(dz)[0]).wait_recv()

        @pl.when(c == 1)
        def _():
            rt_all[r] = rt[N_Z - 1]

            def ra_start(i, carry):
                to = lax.rem(r + i, N_DP)
                remote(rt_all.at[r], rt_all.at[r], ra_s.at[0], ra_r.at[0], to, ep).start()
                return carry

            lax.fori_loop(1, N_DP, ra_start, 0)

    valv = vals[...]
    steps = [(p, dz) for p in range(n_pieces) for dz in order]
    for n, (p, dz) in enumerate(steps):
        zz, _ = peer(dz)
        first, width = PIECES[p]
        block = mm(valv, op[:, pl.ds(pl.multiple_of(zz * COLS + first, 128), width)])
        top, bottom = block[:HALF], block[HALF:]
        own[p][zz] = jnp.where(c == 0, top, bottom)
        px_send[p][zz] = jnp.where(c == 0, bottom, top).astype(BF)
        px_copy(p, zz).start()
        if n >= LAG:
            pair_sum(*steps[n - LAG])
        if n == 4:
            spread_routes()
    for step in steps[len(steps) - LAG:]:
        pair_sum(*step)

    @pl.when(c == 1)
    def _():
        ra_all().wait_recv()
        rt_last[...] = rt_all[plan_s[r]]

    @pl.when(c == 0)
    def _():
        rt_last[...] = rt[N_Z - 1]

    slot = lax.broadcasted_iota(jnp.int32, (N_DP * SLOTS, HALF), 0)
    row = lax.broadcasted_iota(jnp.int32, (N_DP * SLOTS, HALF), 1)
    expert = slot // SLOTS
    t_row = lax.broadcasted_iota(jnp.int32, (HALF, HALF), 0)
    t_col = lax.broadcasted_iota(jnp.int32, (HALF, HALF), 1)
    earlier = jnp.where((t_row // SPAN == t_col // SPAN) & (t_row < t_col), 1.0, 0.0).astype(BF)
    same = (slot // 2) % N_Z == row // SPAN

    def slot_matrix(final):
        blocks = [rt[i] for i in range(N_Z - 1)] + [final]
        first = jnp.concatenate([block[0:1, :] for block in blocks], axis=1)
        second = jnp.concatenate([block[1:2, :] for block in blocks], axis=1)
        named = jnp.where((first == expert) | (second == expert), 1.0, 0.0)
        before = mm(named.astype(BF), earlier)
        return jnp.where(same & (before == (slot % 2).astype(F32)), named, 0.0)

    slots_t = slot_matrix(rt_last[...]).astype(BF)

    def a_copy(p, to, dz):
        return remote(
            a_send[p].at[to], x[p].at[z, c, r], a_s.at[p, dz], a_r.at[p, z], to, peer(dz)[1])

    for p, (first, width) in enumerate(PIECES):
        total = own[p][z]
        for dz in (1, 3, 2):
            zz, to = peer(dz)
            remote(rs_send[p].at[zz], rs_recv[p].at[zz], rs_s.at[p, dz], rs_r.at[p, zz], r, to).wait_recv()
            total = total + rs_recv[p][zz].astype(F32)
        a_send[p][...] = mm(slots_t, total.astype(BF)).reshape(N_DP, SLOTS, width).astype(BF)
        if p == 0:
            pl.semaphore_wait(in_sem, 3)

        def a_start(i, carry):
            to = lax.rem(r + i, N_DP)
            for dz in range(N_Z):
                a_copy(p, to, dz).start()
            return carry

        for dz in (1, 2, 3):
            a_copy(p, r, dz).start()
        lax.fori_loop(1, N_DP, a_start, 0)
        x[p][z, c, r] = a_send[p][r]

    slots = slot_matrix(rt[N_Z - 1]).T.astype(BF)

    half = N_DP * SLOTS
    to_row = lax.broadcasted_iota(jnp.int32, (2 * half, 2 * half), 0)
    from_row = lax.broadcasted_iota(jnp.int32, (2 * half, 2 * half), 1)
    rank = (to_row % half) // SLOTS
    partner = jnp.zeros_like(rank)
    for i in range(N_DP):
        partner = jnp.where(rank == i, plan_s[i], partner)
    moves = (to_row >= half) & (to_row % SLOTS >= SLOTS - 2)
    wanted = to_row + jnp.where(moves, (partner - rank) * SLOTS, 0)
    swap[...] = jnp.where(from_row == wanted, 1.0, 0.0).astype(BF)

    def a_wait(p, zz, count):
        part = x[p].at[zz, c, pl.ds(0, count)]
        remote(part, part, a_s.at[p, 0], a_r.at[p, zz], r, sib).wait_recv()

    def h_copy(p, zz, cc):
        return remote(x[p].at[zz, cc], x[p].at[zz, cc], h_s.at[p, zz], h_r.at[p, zz], r, sib)

    for i in (5, 6, 7, 8):
        load[i].wait()
    square[...] = jnp.zeros_like(square)
    gate[...] = jnp.zeros_like(gate)
    upper[...] = jnp.zeros_like(upper)
    logit[...] = jnp.zeros_like(logit)

    def expert_chunk(p, zz):
        first, width = PIECES[p]
        h_copy(p, zz, 1 - c).wait_recv()
        at = pl.multiple_of(zz * COLS + first, 128)
        m = x[p][zz].astype(F32).reshape(2 * half, width)
        square[...] += jnp.sum(m * m, axis=1, keepdims=True)
        xin = (m * gain[pl.ds(at, width)].reshape(1, width)).astype(BF)
        gate[...] += mm(xin, gu[0, pl.ds(at, width)])
        upper[...] += mm(xin, gu[1, pl.ds(at, width)])
        logit[...] += lax.dot_general(
            xin, router[:, pl.ds(at, width)], (((1,), (1,)), ((), ())), preferred_element_type=F32)

    previous = None
    for p in range(n_pieces):
        for dz in (0, 1, 3, 2):
            zz, _ = peer(dz)
            a_wait(p, zz, N_DP if dz else N_DP - 1)
            h_copy(p, zz, c).start()
            if previous is not None:
                expert_chunk(*previous)
            previous = (p, zz)
    expert_chunk(*previous)

    scale = lax.rsqrt(square[...] * (1.0 / D) + norm_eps)
    pick = lax.broadcasted_iota(jnp.int32, logit.shape, 1) == r
    chosen = jax.nn.sigmoid(jnp.sum(jnp.where(pick, logit[...], 0.0), axis=1, keepdims=True) * scale)
    swapv = swap[...]
    hidv = (jax.nn.silu(gate[...] * scale) * (upper[...] * scale) * chosen).astype(BF)
    hidv = mm(swapv, hidv).astype(BF)

    def ox_copy(zz):
        return remote(ox_send.at[zz], ox_recv.at[zz], ox_s.at[zz], ox_r.at[zz], r, sib)

    def out_sum(dz):
        zz, _ = peer(dz)
        ox_copy(zz).wait_recv()
        total = o_own[zz] + ox_recv[zz].astype(F32)
        if dz == 0:
            total = total + residual[...]
        b_send[zz] = total.reshape(N_DP, SLOTS, COLS).astype(BF)

        def b_start(i, carry):
            to = lax.rem(r + i, N_DP)
            remote(b_send.at[zz, to], b_recv.at[zz, r], b_s.at[zz], b_r.at[zz], to, ep).start()
            return carry

        lax.fori_loop(1, N_DP, b_start, 0)
        b_recv[zz, r] = b_send[zz, r]

    def t_start(i, carry):
        to = lax.rem(r + i, N_DP)
        remote(t_send.at[to], t_recv.at[r], t_s.at[0], t_r.at[0], to, ep).start()
        return carry

    for n, dz in enumerate(order):
        zz, _ = peer(dz)
        block = mm(hidv, dn[:, pl.ds(pl.multiple_of(zz * COLS, 128), COLS)])
        top, bottom = block[:half], block[half:]
        ox_send[zz] = jnp.where(c == 0, bottom, top).astype(BF)
        ox_copy(zz).start()
        o_own[zz] = jnp.where(c == 0, top, bottom)
        if n:
            out_sum(order[n - 1])
        if n == 1:
            column = lax.broadcasted_iota(jnp.int32, (2 * half, EXTRA), 1)
            high = chosen.astype(BF).astype(F32)
            tail = jnp.where(column == 0, high, jnp.where(column == 1, chosen - high, 0.0)).astype(BF)
            tail = mm(swapv, tail)
            chosen = tail[:, 0:1] + tail[:, 1:2]
            t_send[...] = jnp.where(c == 0, tail[:half], tail[half:]).reshape(N_DP, SLOTS, EXTRA).astype(BF)
            lax.fori_loop(1, N_DP, t_start, 0)
            t_recv[r] = t_send[r]
        if n == 2:
            swap_half = jnp.where(c == 0, swapv[:half, :half], swapv[half:, half:])
            mine = jnp.where(c == 0, chosen[:half], chosen[half:]) * (1.0 / route_scale)
            for p, (first, width) in enumerate(PIECES):
                rows_in = x[p][z, c].astype(F32).reshape(half, width).astype(BF)
                residual[:, first:first + width] = mm(swap_half, rows_in) * mine
    out_sum(order[-1])

    def f_copy(dz, zz):
        to_z, to = peer(dz)
        return remote(
            f_send.at[zz, to_z], f_recv.at[z, zz], f_s.at[zz, dz], f_r.at[z, zz], r, to)

    def b_all(zz):
        part = b_recv.at[zz, pl.ds(0, N_DP - 1)]
        return remote(part, part, b_s.at[zz], b_r.at[zz], r, sib)

    for dz in order:
        zz, _ = peer(dz)
        b_all(zz).wait_recv()
        joined = mm(slots, b_recv[zz].astype(F32).reshape(half, COLS).astype(BF))
        f_send[zz] = joined.reshape(N_Z, SPAN, COLS).astype(BF)
        for to in (2, 1, 3):
            f_copy(to, zz).start()
    t_part = t_recv.at[pl.ds(0, N_DP - 1)]
    remote(t_part, t_part, t_s.at[0], t_r.at[0], r, sib).wait_recv()
    weight[...] = mm(slots, t_recv[...].astype(F32).reshape(half, EXTRA).astype(BF)).reshape(
        N_Z, SPAN, EXTRA)
    mine = weight[z]
    factor = route_scale / (mine[:, 0:1] + mine[:, 1:2])

    def store(zz):
        columns = pl.ds(pl.multiple_of(zz * COLS, 128), COLS)
        return pltpu.make_async_copy(result.at[zz], out.at[:, columns], o_sem.at[zz])

    for dz in order:
        zz, _ = peer(dz)
        total = f_send[zz, z].astype(F32)
        for frm in (1, 3, 2):
            from_z, _ = peer(frm)
            remote(
                f_send.at[zz, z], f_recv.at[from_z, zz], f_s.at[zz, frm], f_r.at[from_z, zz], r, sib
            ).wait_recv()
            total = total + f_recv[from_z, zz].astype(F32)
        result[zz] = (total * factor).astype(BF)
        store(zz).start()

    for i in range(N_Z):
        store(i).wait()
    for dz in range(N_Z):
        zz, to = peer(dz)
        count = N_DP if dz else N_DP - 1
        b_all(zz).wait_send()
        for p in range(n_pieces):
            part = a_send[p].at[pl.ds(0, count)]
            remote(part, part, a_s.at[p, dz], a_r.at[p, zz], r, sib).wait_send()
            px_copy(p, zz).wait_send()
            h_copy(p, zz, c).wait_send()
            if dz:
                rs_copy(p, dz).wait_send()
        ox_copy(zz).wait_send()
        if dz:
            rt_copy(dz, z).wait_send()
            for chunk in range(N_Z):
                f_copy(dz, chunk).wait_send()
    remote(t_part, t_part, t_s.at[0], t_r.at[0], r, sib).wait_send()

    @pl.when(c == 1)
    def _():
        ra_all().wait_send()


def per_device(
    queries_c, queries_r, latents, key_rope, value_up, out_proj, norm_gain, router, gate_up, down,
    routes, lengths, plan,
):
    any_spec = pl.BlockSpec(memory_space=pl.ANY)
    vm = pltpu.VMEM
    dma = pltpu.SemaphoreType.DMA
    half = N_DP * SLOTS
    scratch = [
        pltpu.SMEM((N_DP,), jnp.int32), pltpu.SMEM((N_DP,), jnp.int32),
        vm((S, HEADS_HERE * LAT), BF), vm((S, HEADS_HERE * ROPE), BF), vm((S, LAT), BF), vm((ROPE, S), BF),
        vm((HEADS_HERE, LAT, VDIM), BF), vm((HEADS_HERE * VDIM, D), BF), vm((D,), F32),
        vm((N_DP, D), BF), vm((2, D, 256), BF), vm((256, D), BF),
        vm((N_Z, 2, SPAN), jnp.int32), vm((N_DP, 2, SPAN), jnp.int32), vm((2, SPAN), jnp.int32),
        vm((S, HEADS_HERE * VDIM), BF),
        vm((2 * half, 256), F32), vm((2 * half, 256), F32), vm((2 * half, N_DP), F32), vm((2 * half, 1), F32),
        vm((2 * half, 2 * half), BF),
        vm((N_Z, half, COLS), F32), vm((half, COLS), F32), vm((N_Z, half, COLS), BF), vm((N_Z, half, COLS), BF),
        vm((N_Z, N_DP, SLOTS, COLS), BF), vm((N_Z, N_DP, SLOTS, COLS), BF),
        vm((N_DP, SLOTS, EXTRA), BF), vm((N_DP, SLOTS, EXTRA), BF),
        vm((N_Z, N_Z, SPAN, COLS), BF), vm((N_Z, N_Z, SPAN, COLS), BF),
        vm((N_Z, SPAN, EXTRA), F32), vm((N_Z, SPAN, COLS), BF),
    ]
    widths = [width for _, width in PIECES]
    n_pieces = len(PIECES)
    scratch += [vm((N_Z, HALF, w), F32) for w in widths]
    for _ in range(4):
        scratch += [vm((N_Z, HALF, w), BF) for w in widths]
    scratch += [vm((N_DP, SLOTS, w), BF) for w in widths]
    scratch += [vm((N_Z, 2, N_DP, SLOTS, w), BF) for w in widths]
    by_piece = dma((n_pieces, 4))
    scratch += [
        dma((11,)), dma((16,)), dma((4,)), pltpu.SemaphoreType.REGULAR, dma((4,)), dma((4,)), dma((1,)), dma((1,)),
        by_piece, by_piece, by_piece, by_piece, by_piece, by_piece, by_piece, by_piece,
        dma((4,)), dma((4,)), dma((4,)), dma((4,)), dma((1,)), dma((1,)), dma((4, 4)), dma((4, 4)),
    ]
    return pl.pallas_call(
        kernel,
        out_shape=jax.ShapeDtypeStruct((SPAN, D), BF),
        in_specs=[any_spec] * 13,
        out_specs=any_spec,
        scratch_shapes=scratch,
        compiler_params=pltpu.CompilerParams(
            collective_id=0, has_side_effects=True, vmem_limit_bytes=56 * 1024 * 1024),
        cost_estimate=pl.CostEstimate(flops=3 * 10**9, bytes_accessed=16 * 10**6, transcendentals=10**6),
    )(
        lengths, plan, queries_c, queries_r, latents, key_rope, value_up, out_proj,
        norm_gain, router.T, gate_up, down, routes.T,
    )


def solution(mesh):
    placed = (
        P("dp", "ep"),
        P("dp", "ep"),
        P("dp", None),
        P(None, "dp"),
        P("ep", None, None),
        P("ep", None),
        P(),
        P(),
        P("dp", None, None, "ep"),
        P("dp", "ep", None),
        P(("dp", "ep"), None),
        P(),
        P(),
    )
    return jax.shard_map(
        per_device, mesh=mesh, in_specs=placed, out_specs=P(("dp", "ep"), None), check_vma=False
    )
```

time: 63.6 us -> 57.9 us (0.910)
  Pallas kernels: 61.9 us -> 56.2 us
    pallas_call x1, Pallas kernels: 61.9 us -> 56.2 us  [per_device(): pl.pallas_call(kernel, out_shape=jax.ShapeDtypeStruct((SPAN, D), BF), in_...]
where the time goes in v4:
time: 57.9 us; the launch traced here: 57.8 us
  Pallas kernels  56.2 us (97%)
  local copies, waits for them, and re-layouts  1.55 us (3%)
    pallas_call x1, Pallas kernels, per_device(): pl.pallas_call(kernel, out_shape=jax.ShapeDtypeStruct((SPAN, D), BF), in_...  56.2 us
    unnamed x1, local copies, waits for them, and re-layouts  1.55 us

profile of v4, /device:TPU:1, one launch (start us, length us, event | category | flops | bytes accessed | tf_op | source)
XLA Modules:
  0.0 57.8 jit_solution(12020288144309455655)
XLA Ops:
  0.0 56.2 %shard_map.127 = bf16[16,3584]{1,0:T(8,128)(2,1)} custom-call(s32[16]{0:T(128)} %lengths_h.1, s32[16]{0:T(128)} %plan_h.1, bf16[128,4096]{1,0:T(8,128)(2,1)} %qc_h.1, bf16[128,512]{1,0:T(8,128)(2,1)} %qr_h.1, bf16[128,512]{1,0:T(8,128)(2,1)} %lat_h.1, bf16[64,128]{1,0:T(8,128)(2,1)} %kr_h.1, bf16[8,512,128]{2,1,0:T(8,128)(2,1)} %vu_h.1, ...), custom_call_target="tpu_custom_call" | custom-call | flops 3000000000 | bytes 16000000 | tf_op jit(solution)/shard_map/pallas_call | solution.py:454
  56.2 1.6 %copy.15 = bf16[16,3584]{1,0:T(8,128)(2,1)} copy(bf16[16,3584]{1,0:T(8,128)(2,1)} %shard_map.127) | data formatting | bytes 229376

commit v5 on v4

--- a/solution.py
+++ b/solution.py
@@ -22,6 +22,7 @@
 COLS = D // N_Z
 SLOTS = 8
 EXTRA = 128
+BACK = ((0, 384), (384, 512))
 LAG = 2
 PIECES = ((0, 384), (384, 512))
 
@@ -51,14 +52,15 @@
     out,
     lengths_s, plan_s, qc, qr, lat, kr, vu, op, gain, router, gu, dn, rt, rt_all, rt_last,
     vals, gate, upper, logit, square, swap,
-    o_own, residual, ox_send, ox_recv, b_send, b_recv, t_send, t_recv, f_send, f_recv, weight, result,
+    residual, c_send, c_recv, d_send, d_recv, e_send, e_recv, b_send, b_recv, t_send, t_recv,
+    f_send, f_recv, weight, result,
     *rest,
 ):
     n_pieces = len(PIECES)
-    own, px_send, px_recv, rs_send, rs_recv, a_send, x = (
-        rest[i * n_pieces:(i + 1) * n_pieces] for i in range(7))
+    own, px_send, px_recv, rs_send, rs_recv, a_send, x, o_own, ox_send, ox_recv = (
+        rest[i * n_pieces:(i + 1) * n_pieces] for i in range(10))
     (l_sem, q_sem, o_sem, in_sem, rt_s, rt_r, ra_s, ra_r, px_s, px_r, rs_s, rs_r, a_s, a_r, h_s, h_r,
-     ox_s, ox_r, b_s, b_r, t_s, t_r, f_s, f_r) = rest[7 * n_pieces:]
+     ox_s, ox_r, b_s, b_r, t_s, t_r, f_s, f_r, c_s, c_r, d_s, d_r, e_s, e_r) = rest[10 * n_pieces:]
     r = lax.axis_index("dp")
     ep = lax.axis_index("ep")
     z = ep // 2
@@ -73,6 +75,9 @@
     def peer(dz):
         zz = lax.rem(z + dz, N_Z)
         return zz, zz * 2 + c
+
+    def other(i):
+        return lax.rem(r + N_DP * N_DP + (1 - 2 * c) * i, N_DP)
 
     barrier = pltpu.get_barrier_semaphore()
 
@@ -169,7 +174,7 @@
             rt_all[r] = rt[N_Z - 1]
 
             def ra_start(i, carry):
-                to = lax.rem(r + i, N_DP)
+                to = other(i)
                 remote(rt_all.at[r], rt_all.at[r], ra_s.at[0], ra_r.at[0], to, ep).start()
                 return carry
 
@@ -234,7 +239,7 @@
             pl.semaphore_wait(in_sem, 3)
 
         def a_start(i, carry):
-            to = lax.rem(r + i, N_DP)
+            to = other(i)
             for dz in range(N_Z):
                 a_copy(p, to, dz).start()
             return carry
@@ -301,72 +306,113 @@
     hidv = (jax.nn.silu(gate[...] * scale) * (upper[...] * scale) * chosen).astype(BF)
     hidv = mm(swapv, hidv).astype(BF)
 
-    def ox_copy(zz):
-        return remote(ox_send.at[zz], ox_recv.at[zz], ox_s.at[zz], ox_r.at[zz], r, sib)
-
-    def out_sum(dz):
+    def ox_copy(p, zz):
+        return remote(ox_send[p].at[zz], ox_recv[p].at[zz], ox_s.at[p, zz], ox_r.at[p, zz], r, sib)
+
+    def c_copy(dz):
+        zz, to = peer(dz)
+        return remote(c_send.at[zz], c_recv.at[z], c_s.at[dz], c_r.at[z], r, to)
+
+    def b_copy(zz, to):
+        return remote(b_send.at[zz, to], b_recv.at[zz, r], b_s.at[zz], b_r.at[zz], to, ep)
+
+    def b_all(zz):
+        part = b_recv.at[zz, pl.ds(0, N_DP - 1)]
+        return remote(part, part, b_s.at[zz], b_r.at[zz], r, sib)
+
+    def d_copy(to):
+        return remote(d_send.at[to], d_recv.at[r], d_s.at[0], d_r.at[0], to, ep)
+
+    def d_all():
+        part = d_recv.at[pl.ds(0, N_DP - 1)]
+        return remote(part, part, d_s.at[0], d_r.at[0], r, sib)
+
+    def to_ranks(make):
+        def start(i, carry):
+            make(other(i)).start()
+            return carry
+
+        lax.fori_loop(1, N_DP, start, 0)
+
+    def out_sum(p, dz):
         zz, _ = peer(dz)
-        ox_copy(zz).wait_recv()
-        total = o_own[zz] + ox_recv[zz].astype(F32)
+        first, width = BACK[p]
+        ox_copy(p, zz).wait_recv()
+        total = o_own[p][zz] + ox_recv[p][zz].astype(F32)
         if dz == 0:
-            total = total + residual[...]
-        b_send[zz] = total.reshape(N_DP, SLOTS, COLS).astype(BF)
-
-        def b_start(i, carry):
-            to = lax.rem(r + i, N_DP)
-            remote(b_send.at[zz, to], b_recv.at[zz, r], b_s.at[zz], b_r.at[zz], to, ep).start()
-            return carry
-
-        lax.fori_loop(1, N_DP, b_start, 0)
-        b_recv[zz, r] = b_send[zz, r]
-
-    def t_start(i, carry):
-        to = lax.rem(r + i, N_DP)
-        remote(t_send.at[to], t_recv.at[r], t_s.at[0], t_r.at[0], to, ep).start()
-        return carry
-
-    for n, dz in enumerate(order):
+            total = total + residual[:, first:first + width]
+        if p == 1:
+            b_send[zz] = total.reshape(N_DP, SLOTS, width).astype(BF)
+            to_ranks(lambda to: b_copy(zz, to))
+            b_recv[zz, r] = b_send[zz, r]
+        elif dz:
+            c_send[zz] = total.astype(BF)
+            c_copy(dz).start()
+        else:
+            o_own[p][zz] = total
+
+    for n, (p, dz) in enumerate(steps):
         zz, _ = peer(dz)
-        block = mm(hidv, dn[:, pl.ds(pl.multiple_of(zz * COLS, 128), COLS)])
+        first, width = BACK[p]
+        block = mm(hidv, dn[:, pl.ds(pl.multiple_of(zz * COLS + first, 128), width)])
         top, bottom = block[:half], block[half:]
-        ox_send[zz] = jnp.where(c == 0, bottom, top).astype(BF)
-        ox_copy(zz).start()
-        o_own[zz] = jnp.where(c == 0, top, bottom)
-        if n:
-            out_sum(order[n - 1])
-        if n == 1:
+        ox_send[p][zz] = jnp.where(c == 0, bottom, top).astype(BF)
+        ox_copy(p, zz).start()
+        o_own[p][zz] = jnp.where(c == 0, top, bottom)
+        if n == 3:
             column = lax.broadcasted_iota(jnp.int32, (2 * half, EXTRA), 1)
             high = chosen.astype(BF).astype(F32)
             tail = jnp.where(column == 0, high, jnp.where(column == 1, chosen - high, 0.0)).astype(BF)
             tail = mm(swapv, tail)
             chosen = tail[:, 0:1] + tail[:, 1:2]
             t_send[...] = jnp.where(c == 0, tail[:half], tail[half:]).reshape(N_DP, SLOTS, EXTRA).astype(BF)
-            lax.fori_loop(1, N_DP, t_start, 0)
-            t_recv[r] = t_send[r]
-        if n == 2:
             swap_half = jnp.where(c == 0, swapv[:half, :half], swapv[half:, half:])
             mine = jnp.where(c == 0, chosen[:half], chosen[half:]) * (1.0 / route_scale)
-            for p, (first, width) in enumerate(PIECES):
-                rows_in = x[p][z, c].astype(F32).reshape(half, width).astype(BF)
-                residual[:, first:first + width] = mm(swap_half, rows_in) * mine
-    out_sum(order[-1])
+            for q, (start, size) in enumerate(PIECES):
+                rows_in = x[q][z, c].astype(F32).reshape(half, size).astype(BF)
+                residual[:, start:start + size] = mm(swap_half, rows_in) * mine
+        if n >= 3:
+            out_sum(*steps[n - 3])
+    for step in steps[len(steps) - 3:]:
+        out_sum(*step)
+
+    total = o_own[0][z]
+    for dz in (1, 3, 2):
+        zz, to = peer(dz)
+        remote(c_send.at[zz], c_recv.at[zz], c_s.at[dz], c_r.at[zz], r, to).wait_recv()
+        total = total + c_recv[zz].astype(F32)
+    d_send[...] = total.reshape(N_DP, SLOTS, BACK[0][1]).astype(BF)
+    to_ranks(d_copy)
+    d_recv[r] = d_send[r]
+
+    def t_copy(to):
+        return remote(t_send.at[to], t_recv.at[r], t_s.at[0], t_r.at[0], to, ep)
+
+    to_ranks(t_copy)
+    t_recv[r] = t_send[r]
 
     def f_copy(dz, zz):
         to_z, to = peer(dz)
         return remote(
             f_send.at[zz, to_z], f_recv.at[z, zz], f_s.at[zz, dz], f_r.at[z, zz], r, to)
 
-    def b_all(zz):
-        part = b_recv.at[zz, pl.ds(0, N_DP - 1)]
-        return remote(part, part, b_s.at[zz], b_r.at[zz], r, sib)
+    def e_copy(dz):
+        to_z, to = peer(dz)
+        return remote(e_send.at[to_z], e_recv.at[z], e_s.at[dz], e_r.at[z], r, to)
 
     for dz in order:
         zz, _ = peer(dz)
         b_all(zz).wait_recv()
-        joined = mm(slots, b_recv[zz].astype(F32).reshape(half, COLS).astype(BF))
-        f_send[zz] = joined.reshape(N_Z, SPAN, COLS).astype(BF)
+        joined = mm(slots, b_recv[zz].astype(F32).reshape(half, BACK[1][1]).astype(BF))
+        f_send[zz] = joined.reshape(N_Z, SPAN, BACK[1][1]).astype(BF)
         for to in (2, 1, 3):
             f_copy(to, zz).start()
+    d_all().wait_recv()
+    joined = mm(slots, d_recv[...].astype(F32).reshape(half, BACK[0][1]).astype(BF))
+    e_send[...] = joined.reshape(N_Z, SPAN, BACK[0][1]).astype(BF)
+    for dz in (2, 1, 3):
+        e_copy(dz).start()
+    e_recv[z] = e_send[z]
     t_part = t_recv.at[pl.ds(0, N_DP - 1)]
     remote(t_part, t_part, t_s.at[0], t_r.at[0], r, sib).wait_recv()
     weight[...] = mm(slots, t_recv[...].astype(F32).reshape(half, EXTRA).astype(BF)).reshape(
@@ -387,7 +433,12 @@
                 f_send.at[zz, z], f_recv.at[from_z, zz], f_s.at[zz, frm], f_r.at[from_z, zz], r, sib
             ).wait_recv()
             total = total + f_recv[from_z, zz].astype(F32)
-        result[zz] = (total * factor).astype(BF)
+        result[zz, :, BACK[1][0]:] = (total * factor).astype(BF)
+    for dz in (0, 1, 3, 2):
+        zz, to = peer(dz)
+        if dz:
+            remote(e_send.at[zz], e_recv.at[zz], e_s.at[dz], e_r.at[zz], r, to).wait_recv()
+        result[zz, :, :BACK[1][0]] = (e_recv[zz].astype(F32) * factor).astype(BF)
         store(zz).start()
 
     for i in range(N_Z):
@@ -400,15 +451,18 @@
             part = a_send[p].at[pl.ds(0, count)]
             remote(part, part, a_s.at[p, dz], a_r.at[p, zz], r, sib).wait_send()
             px_copy(p, zz).wait_send()
+            ox_copy(p, zz).wait_send()
             h_copy(p, zz, c).wait_send()
             if dz:
                 rs_copy(p, dz).wait_send()
-        ox_copy(zz).wait_send()
         if dz:
             rt_copy(dz, z).wait_send()
+            c_copy(dz).wait_send()
+            e_copy(dz).wait_send()
             for chunk in range(N_Z):
                 f_copy(dz, chunk).wait_send()
     remote(t_part, t_part, t_s.at[0], t_r.at[0], r, sib).wait_send()
+    d_all().wait_send()
 
     @pl.when(c == 1)
     def _():
@@ -432,10 +486,12 @@
         vm((S, HEADS_HERE * VDIM), BF),
         vm((2 * half, 256), F32), vm((2 * half, 256), F32), vm((2 * half, N_DP), F32), vm((2 * half, 1), F32),
         vm((2 * half, 2 * half), BF),
-        vm((N_Z, half, COLS), F32), vm((half, COLS), F32), vm((N_Z, half, COLS), BF), vm((N_Z, half, COLS), BF),
-        vm((N_Z, N_DP, SLOTS, COLS), BF), vm((N_Z, N_DP, SLOTS, COLS), BF),
+        vm((half, COLS), F32), vm((N_Z, half, BACK[0][1]), BF), vm((N_Z, half, BACK[0][1]), BF),
+        vm((N_DP, SLOTS, BACK[0][1]), BF), vm((N_DP, SLOTS, BACK[0][1]), BF),
+        vm((N_Z, SPAN, BACK[0][1]), BF), vm((N_Z, SPAN, BACK[0][1]), BF),
+        vm((N_Z, N_DP, SLOTS, BACK[1][1]), BF), vm((N_Z, N_DP, SLOTS, BACK[1][1]), BF),
         vm((N_DP, SLOTS, EXTRA), BF), vm((N_DP, SLOTS, EXTRA), BF),
-        vm((N_Z, N_Z, SPAN, COLS), BF), vm((N_Z, N_Z, SPAN, COLS), BF),
+        vm((N_Z, N_Z, SPAN, BACK[1][1]), BF), vm((N_Z, N_Z, SPAN, BACK[1][1]), BF),
         vm((N_Z, SPAN, EXTRA), F32), vm((N_Z, SPAN, COLS), BF),
     ]
     widths = [width for _, width in PIECES]
@@ -445,11 +501,16 @@
         scratch += [vm((N_Z, HALF, w), BF) for w in widths]
     scratch += [vm((N_DP, SLOTS, w), BF) for w in widths]
     scratch += [vm((N_Z, 2, N_DP, SLOTS, w), BF) for w in widths]
+    backs = [width for _, width in BACK]
+    scratch += [vm((N_Z, half, w), F32) for w in backs]
+    for _ in range(2):
+        scratch += [vm((N_Z, half, w), BF) for w in backs]
     by_piece = dma((n_pieces, 4))
     scratch += [
         dma((11,)), dma((16,)), dma((4,)), pltpu.SemaphoreType.REGULAR, dma((4,)), dma((4,)), dma((1,)), dma((1,)),
         by_piece, by_piece, by_piece, by_piece, by_piece, by_piece, by_piece, by_piece,
-        dma((4,)), dma((4,)), dma((4,)), dma((4,)), dma((1,)), dma((1,)), dma((4, 4)), dma((4, 4)),
+        by_piece, by_piece, dma((4,)), dma((4,)), dma((1,)), dma((1,)), dma((4, 4)), dma((4, 4)),
+        dma((4,)), dma((4,)), dma((1,)), dma((1,)), dma((4,)), dma((4,)),
     ]
     return pl.pallas_call(
         kernel,

time: 57.9 us -> 54.9 us (0.948); the launches traced: 57.8 us -> 54 us
  Pallas kernels: 56.2 us -> 52.4 us
    pallas_call x1, Pallas kernels: 56.2 us -> 52.4 us  [per_device(): pl.pallas_call(kernel, out_shape=jax.ShapeDtypeStruct((SPAN, D), BF), in_...]
where the time goes in v5:
time: 54.9 us; the launch traced here: 54 us
  Pallas kernels  52.4 us (95%)
  local copies, waits for them, and re-layouts  1.55 us (3%)
    pallas_call x1, Pallas kernels, per_device(): pl.pallas_call(kernel, out_shape=jax.ShapeDtypeStruct((SPAN, D), BF), in_...  52.4 us
    unnamed x1, local copies, waits for them, and re-layouts  1.55 us

profile of v5, /device:TPU:1, one launch (start us, length us, event | category | flops | bytes accessed | tf_op | source)
XLA Modules:
  0.0 54.0 jit_solution(17574871713188698014)
XLA Ops:
  0.0 52.4 %shard_map.127 = bf16[16,3584]{1,0:T(8,128)(2,1)} custom-call(s32[16]{0:T(128)} %lengths_h.1, s32[16]{0:T(128)} %plan_h.1, bf16[128,4096]{1,0:T(8,128)(2,1)} %qc_h.1, bf16[128,512]{1,0:T(8,128)(2,1)} %qr_h.1, bf16[128,512]{1,0:T(8,128)(2,1)} %lat_h.1, bf16[64,128]{1,0:T(8,128)(2,1)} %kr_h.1, bf16[8,512,128]{2,1,0:T(8,128)(2,1)} %vu_h.1, ...), custom_call_target="tpu_custom_call" | custom-call | flops 3000000000 | bytes 16000000 | tf_op jit(solution)/shard_map/pallas_call | solution.py:515
  52.4 1.6 %copy.15 = bf16[16,3584]{1,0:T(8,128)(2,1)} copy(bf16[16,3584]{1,0:T(8,128)(2,1)} %shard_map.127) | data formatting | bytes 229376

commit v6 on v5

--- a/solution.py
+++ b/solution.py
@@ -238,15 +238,25 @@
         if p == 0:
             pl.semaphore_wait(in_sem, 3)
 
-        def a_start(i, carry):
-            to = other(i)
-            for dz in range(N_Z):
-                a_copy(p, to, dz).start()
-            return carry
-
-        for dz in (1, 2, 3):
+        def to_plane(planes):
+            def a_start(i, carry):
+                to = other(i)
+                for dz in planes:
+                    a_copy(p, to, dz).start()
+                return carry
+
+            lax.fori_loop(1, N_DP, a_start, 0)
+
+        to_plane((0,))
+        for dz in (1,):
             a_copy(p, r, dz).start()
-        lax.fori_loop(1, N_DP, a_start, 0)
+        to_plane((1,))
+        for dz in (3,):
+            a_copy(p, r, dz).start()
+        to_plane((3,))
+        for dz in (2,):
+            a_copy(p, r, dz).start()
+        to_plane((2,))
         x[p][z, c, r] = a_send[p][r]
 
     slots = slot_matrix(rt[N_Z - 1]).T.astype(BF)

time: 54.9 us -> 54.4 us (level); the launches traced: 54 us -> 54.2 us
  no operation moved by 1% of the time
where the time goes in v6:
time: 54.4 us; the launch traced here: 54.2 us
  Pallas kernels  52.7 us (97%)
  local copies, waits for them, and re-layouts  1.55 us (3%)
    pallas_call x1, Pallas kernels, per_device(): pl.pallas_call(kernel, out_shape=jax.ShapeDtypeStruct((SPAN, D), BF), in_...  52.7 us
    unnamed x1, local copies, waits for them, and re-layouts  1.55 us

profile of v6, /device:TPU:1, one launch (start us, length us, event | category | flops | bytes accessed | tf_op | source)
XLA Modules:
  0.0 54.2 jit_solution(14129052221320779065)
XLA Ops:
  0.0 52.7 %shard_map.127 = bf16[16,3584]{1,0:T(8,128)(2,1)} custom-call(s32[16]{0:T(128)} %lengths_h.1, s32[16]{0:T(128)} %plan_h.1, bf16[128,4096]{1,0:T(8,128)(2,1)} %qc_h.1, bf16[128,512]{1,0:T(8,128)(2,1)} %qr_h.1, bf16[128,512]{1,0:T(8,128)(2,1)} %lat_h.1, bf16[64,128]{1,0:T(8,128)(2,1)} %kr_h.1, bf16[8,512,128]{2,1,0:T(8,128)(2,1)} %vu_h.1, ...), custom_call_target="tpu_custom_call" | custom-call | flops 3000000000 | bytes 16000000 | tf_op jit(solution)/shard_map/pallas_call | solution.py:525
  52.7 1.6 %copy.15 = bf16[16,3584]{1,0:T(8,128)(2,1)} copy(bf16[16,3584]{1,0:T(8,128)(2,1)} %shard_map.127) | data formatting | bytes 229376
